TPU v7x, 512 devices: a whole 4x8x8 slice. The times are simulated.
512 devices in a mesh: gx: 64 (over x, y, z_hi), gy: 8 (over z_lo, core).
Axes of the slice: x: 4, y: 8, z: 8 (z_hi: 2, z_lo: 4; z = z_hi * 4 + z_lo), core: 2. Of those that a mesh axis runs over, the one named last changes fastest.
Arguments:
- displacement: float32 [3, 128, 256, 256], P(None, 'gx', 'gy'), may hold values from -6 to 6
- load: float32 [3, 128, 256, 256], P(None, 'gx', 'gy'), may hold values from -120 to 120
- element_phase: int32 [128, 256, 256], P('gx', 'gy'), may hold values from 0 to 2
- element_modulus: float32 [128, 256, 256], P('gx', 'gy'), may hold values from 1 to 10
- stiffness: float32 [3, 8, 8, 3, 3], replicated, as said below
Outputs:
- relaxed: float32 [3, 128, 256, 256], P(None, 'gx', 'gy')
Inputs may be any that keep to these rules, and one draw needn't show every extreme that they name: For every phase and corner c, stiffness[ph, c, c] has diagonal entries between 2 and 3 and other entries of magnitude at most 0.3.
All inputs are finite; a program needn't handle non-finite values.
Results may differ from a plain program's by a relative error of at most 0.0001.
Values sent between devices are 32-bit elements; how exact they have to be, the bound alone decides.
No kernel may reach another device: no remote copies, remote signals or barrier semaphores. Data moves between devices by JAX's collectives and lax.ppermute only.
A program may use at most 64 MiB of HBM per device.

v0:
```python
import jax
import jax.numpy as jnp
import numpy as np
from jax import lax
from jax.sharding import PartitionSpec as P

corner_list = tuple(
    ((first, second, third) for first in (0, 1) for second in (0, 1) for third in (0, 1))
)
offset_list = tuple(
    (
        (first, second, third)
        for first in (-1, 0, 1)
        for second in (-1, 0, 1)
        for third in (-1, 0, 1)
    )
)
highest = lax.Precision.HIGHEST


def shifted(x, axis, by):
    devices = lax.axis_size(axis)
    return lax.ppermute(x, axis, [(i, (i + by) % devices) for i in range(devices)])


def coupling_selector():
    selector = np.zeros((27, 8, 8), np.float32)
    for index, offset in enumerate(offset_list):
        for source, corner in enumerate(corner_list):
            target = tuple((left + right for left, right in zip(corner, offset)))
            if target in corner_list:
                selector[index, source, corner_list.index(target)] = 1.0
    return selector


def split_parity(array):
    leading = array.shape[:-3]
    size_x, size_y, size_z = array.shape[-3:]
    count = len(leading)
    shaped = array.reshape(leading + (size_x // 2, 2, size_y // 2, 2, size_z // 2, 2))
    order = tuple(range(count)) + (count + 1, count + 3, count + 5, count, count + 2, count + 4)
    return shaped.transpose(order)


def merge_parity(parted):
    moved = parted.transpose((0, 4, 1, 5, 2, 6, 3))
    shape = parted.shape
    return moved.reshape((shape[0], shape[4] * 2, shape[5] * 2, shape[6] * 2))


def solve_blocks(matrix, right):
    m00, m01, m02 = (matrix[0, 0], matrix[0, 1], matrix[0, 2])
    m10, m11, m12 = (matrix[1, 0], matrix[1, 1], matrix[1, 2])
    m20, m21, m22 = (matrix[2, 0], matrix[2, 1], matrix[2, 2])
    c00 = m11 * m22 - m12 * m21
    c01 = m12 * m20 - m10 * m22
    c02 = m10 * m21 - m11 * m20
    c10 = m02 * m21 - m01 * m22
    c11 = m00 * m22 - m02 * m20
    c12 = m01 * m20 - m00 * m21
    c20 = m01 * m12 - m02 * m11
    c21 = m02 * m10 - m00 * m12
    c22 = m00 * m11 - m01 * m10
    determinant = m00 * c00 + m01 * c01 + m02 * c02
    first = (c00 * right[0] + c10 * right[1] + c20 * right[2]) / determinant
    second = (c01 * right[0] + c11 * right[1] + c21 * right[2]) / determinant
    third = (c02 * right[0] + c12 * right[1] + c22 * right[2]) / determinant
    return jnp.stack([first, second, third], axis=0)


def pick_view(stored, parity, offset, width_x, width_y):
    spots = tuple((bit + step for bit, step in zip(parity, offset)))
    which = tuple((spot % 2 for spot in spots))
    moves = tuple((spot // 2 for spot in spots))
    holder, base_x, base_y = stored[which[0], which[1]]
    start_x = base_x + moves[0]
    start_y = base_y + moves[1]
    window = holder[:, which[2], start_x : start_x + width_x, start_y : start_y + width_y]
    if moves[2] < 0:
        window = jnp.concatenate([window[..., -1:], window[..., :-1]], axis=-1)
    return window


def split_update(fields, weight_map, load_part, coeff_table, parity, width_x, width_y):
    wstack = jnp.stack(
        [
            pick_view(weight_map, parity, tuple((-entry for entry in corner)), width_x, width_y)
            for corner in corner_list
        ],
        axis=1,
    )
    wflat = wstack.reshape((wstack.shape[0] * 8,) + wstack.shape[2:])
    diag_table = coeff_table[13]
    off_table = jnp.concatenate([coeff_table[:13], coeff_table[14:]], axis=0)
    diagonal = jnp.tensordot(diag_table, wflat, axes=1, precision=highest)
    coupled = jnp.tensordot(off_table, wflat, axes=1, precision=highest)
    neighbours = jnp.stack(
        [
            pick_view(fields, parity, offset, width_x, width_y)
            for offset in offset_list
            if offset != (0, 0, 0)
        ],
        axis=0,
    )
    accumulated = jnp.einsum("tijxyz,tjxyz->ixyz", coupled, neighbours, precision=highest)
    return solve_blocks(diagonal, load_part - accumulated)


def finish_rows(plane_zero, plane_one, row_zero, row_one):
    stored = {}
    for bit_x, holder, rows in ((0, plane_zero, row_zero), (1, plane_one, row_one)):
        stored[bit_x, 0] = (holder[:, 0], bit_x, 0)
        stored[bit_x, 1] = (jnp.concatenate([rows[:, :, :, None], holder[:, 1]], axis=3), bit_x, 1)
    return stored


def on_device(displacement, load, element_phase, element_modulus, stiffness):
    width_x = displacement.shape[1] // 2
    width_y = displacement.shape[2] // 2
    phases = stiffness.shape[0]
    phase_ids = jnp.arange(phases, dtype=jnp.int32)
    weights = jnp.where(
        element_phase[None] == phase_ids[:, None, None, None],
        element_modulus[None],
        jnp.zeros_like(element_modulus)[None],
    )
    coeff_table = jnp.einsum(
        "tcd,pcdij->tijpc", jnp.asarray(coupling_selector()), stiffness, precision=highest
    ).reshape(27, 3, 3, phases * 8)
    split_disp = split_parity(displacement)
    split_weight = split_parity(weights)
    split_load = split_parity(load)
    rim_disp, rim_weight = shifted(
        (split_disp[:, 1, :, :, width_x - 1], split_weight[:, 1, :, :, width_x - 1]), "gx", 1
    )
    disp_zero = split_disp[:, 0]
    disp_one = jnp.concatenate([rim_disp[:, :, :, None], split_disp[:, 1]], axis=3)
    weight_zero = split_weight[:, 0]
    weight_one = jnp.concatenate([rim_weight[:, :, :, None], split_weight[:, 1]], axis=3)
    row_dz, row_do, row_wz, row_wo = shifted(
        (
            disp_zero[:, 1, :, :, width_y - 1],
            disp_one[:, 1, :, :, width_y - 1],
            weight_zero[:, 1, :, :, width_y - 1],
            weight_one[:, 1, :, :, width_y - 1],
        ),
        "gy",
        1,
    )
    fields = finish_rows(disp_zero, disp_one, row_dz, row_do)
    weight_map = finish_rows(weight_zero, weight_one, row_wz, row_wo)
    first_parity = (0, 0, 0)
    first_new = split_update(
        fields, weight_map, split_load[:, 0, 0, 0], coeff_table, first_parity, width_x, width_y
    )
    holder, base_x, base_y = fields[0, 0]
    fields[0, 0] = (holder.at[:, 0].set(first_new), base_x, base_y)
    rim_zero, rim_one = shifted((fields[0, 0][0][:, :, 0], fields[0, 1][0][:, :, 0]), "gx", -1)
    for bit_y, rim_plane in ((0, rim_zero), (1, rim_one)):
        holder, base_x, base_y = fields[0, bit_y]
        fields[0, bit_y] = (
            jnp.concatenate([holder, rim_plane[:, :, None]], axis=2),
            base_x,
            base_y,
        )
    second_new = split_update(
        fields, weight_map, split_load[:, 1, 0, 0], coeff_table, (1, 0, 0), width_x, width_y
    )
    merged = split_disp.at[:, 0, 0, 0].set(first_new).at[:, 1, 0, 0].set(second_new)
    return merge_parity(merged)


def solution(mesh):
    in_specs = (
        P(None, "gx", "gy", None),
        P(None, "gx", "gy", None),
        P("gx", "gy", None),
        P("gx", "gy", None),
        P(),
    )
    out_specs = P(None, "gx", "gy", None)
    return jax.shard_map(
        on_device, mesh=mesh, in_specs=in_specs, out_specs=out_specs, check_vma=False
    )
```

profile of v0, /device:TPU:1, one launch (start us, length us, event | category | flops | bytes accessed | tf_op | source)
XLA Modules:
  0.0 141.9 jit_solution(13716980471390615608)
XLA Ops:
  0.0 6.3 %broadcast_in_dim.45 = f32[2,16,2,128,2]{4,3,2,1,0:T(8,128)} reshape(f32[2,32,256]{2,1,0:T(8,128)} %param.15) | data formatting | bytes 131072 | tf_op jit(solution)/shard_map/jit(_where)/broadcast_in_dim | solution.py:122
  6.3 2.9 %copy.178 = f32[2,16,2,128,2]{3,1,4,2,0:T(8,128)S(1)} copy(f32[2,16,2,128,2]{4,3,2,1,0:T(8,128)} %broadcast_in_dim.45) | data formatting | bytes 131072 | tf_op jit(solution)/shard_map/jit(_where)/broadcast_in_dim | solution.py:122
  9.2 5.5 %eq.22 = s32[2,16,2,128,2]{4,3,2,1,0:T(8,128)} reshape(s32[2,32,256]{2,1,0:T(8,128)S(1)} %copy-done.3) | data formatting | bytes 131072 | tf_op jit(solution)/shard_map/eq | solution.py:123
  14.7 2.9 %copy.177 = s32[2,16,2,128,2]{3,1,4,2,0:T(8,128)S(1)} copy(s32[2,16,2,128,2]{4,3,2,1,0:T(8,128)} %eq.22) | data formatting | bytes 131072 | tf_op jit(solution)/shard_map/eq | solution.py:123
  17.6 11.5 %collective-permute-start.1 = (f32[3,2,2,16,128]{4,3,0,2,1:T(8,128)S(1)}, f32[3,2,2,16,128]{4,3,0,2,1:T(8,128)S(1)}, u32[]{:S(2)}, u32[]{:S(2)}) collective-permute-start(f32[3,2,2,16,128]{4,3,0,2,1:T(8,128)S(1)} %get-tuple-element.53), channel_id=1, source_target_pairs={{0,8},{8,16},{16,24},{24,32},{32,40},{40,48},{48,56},{56,64},{64,7... | collective-permute-start | bytes 294920 | tf_op jit(solution)/shard_map/ppermute | solution.py:23
  29.1 3.9 %collective-permute-start = (f32[3,2,1,128]{3,1,0,2:T(2,128)S(1)}, f32[3,2,1,128]{3,1,0,2:T(2,128)S(1)}, u32[]{:S(2)}, u32[]{:S(2)}) collective-permute-start(f32[3,2,1,128]{3,1,0,2:T(2,128)S(1)} %bitcast.606), channel_id=1, source_target_pairs={{0,1},{1,2},{2,3},{3,4},{4,5},{5,6},{6,7},{7,0},{8,9},{9,10},{10,1... | collective-permute-start | bytes 9224 | tf_op jit(solution)/shard_map/ppermute | solution.py:23
  33.1 13.9 %reshape.1427 = f32[3,1,2,16,2,128,2]{6,5,4,3,2,0,1:T(8,128)} reshape(f32[3,2,32,256]{3,2,1,0:T(8,128)S(1)} %copy-done.1) | data formatting | bytes 393216 | tf_op jit(solution)/shard_map/reshape | solution.py:40
  47.1 7.6 %copy.174 = f32[3,1,2,16,2,128,2]{5,3,0,6,4,1,2:T(8,128)S(1)} copy(f32[3,1,2,16,2,128,2]{6,5,4,3,2,0,1:T(8,128)} %reshape.1427) | data formatting | bytes 393216 | tf_op jit(solution)/shard_map/reshape | solution.py:40
  54.7 2.1 %collective-permute-start.5 = (f32[3,2,1,128]{3,1,0,2:T(2,128)S(1)}, f32[3,2,1,128]{3,1,0,2:T(2,128)S(1)}, u32[]{:S(2)}, u32[]{:S(2)}) collective-permute-start(f32[3,2,1,128]{3,1,0,2:T(2,128)S(1)} %bitcast.608), channel_id=1, source_target_pairs={{0,1},{1,2},{2,3},{3,4},{4,5},{5,6},{6,7},{7,0},{8,9},{9,10},{10,1... | collective-permute-start | bytes 9224 | tf_op jit(solution)/shard_map/ppermute | solution.py:23
  56.8 1.9 %collective-permute-start.3 = (f32[3,2,2,16,128]{4,3,0,2,1:T(8,128)S(1)}, f32[3,2,2,16,128]{4,3,0,2,1:T(8,128)S(1)}, u32[]{:S(2)}, u32[]{:S(2)}) collective-permute-start(f32[3,2,2,16,128]{4,3,0,2,1:T(8,128)S(1)} %get-tuple-element.47), channel_id=1, source_target_pairs={{0,8},{8,16},{16,24},{24,32},{32,40},{40,48},{48,56},{56,64},{64,7... | collective-permute-start | bytes 294920 | tf_op jit(solution)/shard_map/ppermute | solution.py:23
  58.8 0.1 slice.676
  58.8 0.6 convolution_bitcast_fusion
  59.4 0.1 fusion.35
  59.6 0.1 constant_dynamic-update-slice_fusion.6
  59.7 0.1 slice.671
  59.8 0.3 copy.176
  60.1 0.1 reshape.1437
  60.2 14.0 %reshape.1429 = f32[3,1,2,16,2,128,2]{6,5,4,3,2,0,1:T(8,128)} reshape(f32[3,2,32,256]{3,2,1,0:T(8,128)S(1)} %copy-done.2) | data formatting | bytes 393216 | tf_op jit(solution)/shard_map/reshape | solution.py:40
  74.2 7.6 %copy.191 = f32[3,1,2,16,2,128,2]{5,3,0,1,6,4,2:T(8,128)S(1)} copy(f32[3,1,2,16,2,128,2]{6,5,4,3,2,0,1:T(8,128)} %reshape.1429) | data formatting | bytes 393216 | tf_op jit(solution)/shard_map/reshape | solution.py:40
  82.0 0.1 slice.680
  82.1 11.5 %collective-permute-start.6 = (f32[3,2,17,128]{3,2,0,1:T(8,128)S(1)}, f32[3,2,17,128]{3,2,0,1:T(8,128)S(1)}, u32[]{:S(2)}, u32[]{:S(2)}) collective-permute-start(f32[3,2,17,128]{3,2,0,1:T(8,128)S(1)} %get-tuple-element.92), channel_id=1, source_target_pairs={{0,504},{8,0},{16,8},{24,16},{32,24},{40,32},{48,40},{56,48},{64,5... | collective-permute-start | bytes 156680 | tf_op jit(solution)/shard_map/ppermute | solution.py:23
  93.6 0.1 constant_dynamic-update-slice_fusion.4
  93.7 1.2 collective-permute-done.6
  95.0 0.1 slice.762
  95.2 4.6 %collective-permute-start.2 = (f32[3,2,2,128]{3,2,1,0:T(2,128)S(1)}, f32[3,2,2,128]{3,2,1,0:T(2,128)S(1)}, u32[]{:S(2)}, u32[]{:S(2)}) collective-permute-start(f32[3,2,2,128]{3,2,1,0:T(2,128)S(1)} %bitcast.604), channel_id=1, source_target_pairs={{0,1},{1,2},{2,3},{3,4},{4,5},{5,6},{6,7},{7,0},{8,9},{9,10},{10,1... | collective-permute-start | bytes 18440 | tf_op jit(solution)/shard_map/ppermute | solution.py:23
  99.9 0.1 slice.687
  100.0 1.9 %collective-permute-start.4 = (f32[3,2,2,128]{3,2,1,0:T(2,128)S(1)}, f32[3,2,2,128]{3,2,1,0:T(2,128)S(1)}, u32[]{:S(2)}, u32[]{:S(2)}) collective-permute-start(f32[3,2,2,128]{3,2,1,0:T(2,128)S(1)} %bitcast.602), channel_id=1, source_target_pairs={{0,1},{1,2},{2,3},{3,4},{4,5},{5,6},{6,7},{7,0},{8,9},{9,10},{10,1... | collective-permute-start | bytes 18440 | tf_op jit(solution)/shard_map/ppermute | solution.py:23
  102.0 0.1 constant_dynamic-update-slice_fusion.2
  102.2 0.1 slice.691
  102.3 0.1 constant_dynamic-update-slice_fusion
  102.4 0.3 convolution_bitcast_fusion.1
  102.8 0.3 collective-permute-done.4
  103.1 0.1 slice.701
  103.2 0.1 constant_dynamic-update-slice_fusion.33
  103.3 0.1 constant_dynamic-update-slice_fusion.30
  103.4 0.1 slice.708
  103.5 0.1 constant_dynamic-update-slice_fusion.27
  103.5 0.1 constant_dynamic-update-slice_fusion.67
  103.7 0.1 constant_dynamic-update-slice_fusion.21
  103.7 0.1 constant_dynamic-update-slice_fusion.19
  103.9 0.1 constant_dynamic-update-slice_fusion.16
  104.0 0.1 constant_dynamic-update-slice_fusion.13
  104.2 0.1 constant_dynamic-update-slice_fusion.10
  104.3 0.2 copy.253
  104.6 0.1 constant_dynamic-update-slice_fusion.38
  104.6 0.1 constant_dynamic-update-slice_fusion.36
  104.7 0.1 constant_dynamic-update-slice_fusion.34
  104.8 0.3 fusion.1
  105.1 2.4 %multiply_reduce_fusion.1 = f32[16,128,3]{1,0,2:T(8,128)S(1)} fusion(f32[16,128,3,26]{1,3,0,2:T(8,128)S(1)} %copy.253, f32[3,8,1,16,128]{4,3,0,2,1:T(8,128)S(1)} %constant_dynamic-update-slice_fusion, f32[13,3,3,24]{0,3,2,1:T(8,128)S(1)} %get-tuple-element.104, f32[13,3,3,24]{0,3,2,1:T(8,128)S(1)} %get-tuple-element.105), kind=kOutput, calls=%fused_computation.1 | convolution fusion | flops 138976752 | bytes 882624 | tf_op jit(solution)/shard_map/dot_general | solution.py:96
  107.7 0.1 constant_dynamic-update-slice_fusion.64
  107.8 0.1 constant_dynamic-update-slice_fusion.61
  107.9 0.1 constant_dynamic-update-slice_fusion.58
  107.9 0.1 constant_dynamic-update-slice_fusion.55
  108.0 0.1 constant_dynamic-update-slice_fusion.53
  108.1 0.1 constant_dynamic-update-slice_fusion.50
  108.2 12.7 %collective-permute-start.7 = (f32[3,2,16,128]{3,2,0,1:T(8,128)S(1)}, f32[3,2,16,128]{3,2,0,1:T(8,128)S(1)}, u32[]{:S(2)}, u32[]{:S(2)}) collective-permute-start(f32[3,2,16,128]{3,2,0,1:T(8,128)S(1)} %bitcast.543), channel_id=1, source_target_pairs={{0,504},{8,0},{16,8},{24,16},{32,24},{40,32},{48,40},{56,48},{64,5... | collective-permute-start | bytes 147464 | tf_op jit(solution)/shard_map/ppermute | solution.py:23
  121.0 0.9 collective-permute-done.7
  121.9 0.1 slice.766
  122.0 0.1 constant_dynamic-update-slice_fusion.47
  122.1 0.1 constant_dynamic-update-slice_fusion.44
  122.2 0.2 copy.254
  122.4 2.4 %multiply_reduce_fusion = f32[16,128,3]{1,0,2:T(8,128)S(1)} fusion(f32[16,128,3,26]{1,3,0,2:T(8,128)S(1)} %copy.254, f32[3,8,1,16,128]{4,3,0,2,1:T(8,128)S(1)} %constant_dynamic-update-slice_fusion.34, f32[13,3,3,24]{0,3,2,1:T(8,128)S(1)} %get-tuple-element.104, f32[13,3,3,24]{0,3,2,1:T(8,128)S(1)} %get-tuple-element.105), kind=kOutput, calls=%fused_computation | convolution fusion | flops 138976752 | bytes 882624 | tf_op jit(solution)/shard_map/dot_general | solution.py:96
  124.9 6.7 %copy.225 = f32[3,1,2,16,2,128,2]{6,5,4,3,2,0,1:T(8,128)} copy(f32[3,1,2,16,2,128,2]{5,3,0,6,4,1,2:T(8,128)S(1)} %bitcast.535) | data formatting | bytes 393216 | tf_op jit(solution)/shard_map/transpose | solution.py:46
  131.6 10.3 %reshape.1435 = f32[3,2,32,256]{3,2,1,0:T(8,128)} reshape(f32[3,1,2,16,2,128,2]{6,5,4,3,2,0,1:T(8,128)} %copy.225) | data formatting | bytes 393216 | tf_op jit(solution)/shard_map/reshape | solution.py:48
  (105 shorter events, 1.5 us)
Async XLA Ops:
  0.0 58.8 %copy-start = (f32[3,8,8,3,3]{2,1,4,3,0:T(8,128)S(1)}, f32[3,8,8,3,3]{2,1,4,3,0:T(8,128)}, u32[]{:S(2)}) copy-start(f32[3,8,8,3,3]{2,1,4,3,0:T(8,128)} %param.16) | copy-start | bytes 20740
  6.3 2.9 %copy-start.3 = (s32[2,32,256]{2,1,0:T(8,128)S(1)}, s32[2,32,256]{2,1,0:T(8,128)}, u32[]{:S(2)}) copy-start(s32[2,32,256]{2,1,0:T(8,128)} %param.14) | copy-start | bytes 196612
  14.7 18.4 %copy-start.1 = (f32[3,2,32,256]{3,2,1,0:T(8,128)S(1)}, f32[3,2,32,256]{3,2,1,0:T(8,128)}, u32[]{:S(2)}) copy-start(f32[3,2,32,256]{3,2,1,0:T(8,128)} %param.12) | copy-start | bytes 589828
  17.6 77.5 %collective-permute-start.1 = (f32[3,2,2,16,128]{4,3,0,2,1:T(8,128)S(1)}, f32[3,2,2,16,128]{4,3,0,2,1:T(8,128)S(1)}, u32[]{:S(2)}, u32[]{:S(2)}) collective-permute-start(f32[3,2,2,16,128]{4,3,0,2,1:T(8,128)S(1)} %get-tuple-element.53), channel_id=1, source_target_pairs={{0,8},{8,16},{16,24},{24,32},{32,40},{40,48},{48,56},{56,64},{64,7... | collective-permute-start | bytes 294920 | tf_op jit(solution)/shard_map/ppermute | solution.py:23
  29.1 52.8 %collective-permute-start = (f32[3,2,1,128]{3,1,0,2:T(2,128)S(1)}, f32[3,2,1,128]{3,1,0,2:T(2,128)S(1)}, u32[]{:S(2)}, u32[]{:S(2)}) collective-permute-start(f32[3,2,1,128]{3,1,0,2:T(2,128)S(1)} %bitcast.606), channel_id=1, source_target_pairs={{0,1},{1,2},{2,3},{3,4},{4,5},{5,6},{6,7},{7,0},{8,9},{9,10},{10,1... | collective-permute-start | bytes 9224 | tf_op jit(solution)/shard_map/ppermute | solution.py:23
  47.0 11.8 %copy-start.4 = (f32[27,8,8,1,1]{0,2,4,3,1:T(8,128)S(1)}, f32[27,8,8,1,1]{0,2,4,3,1:T(8,128)}, u32[]{:S(2)}) copy-start(f32[27,8,8,1,1]{0,2,4,3,1:T(8,128)} %constant.103) | copy-start | bytes 20740
  54.6 5.6 %copy-start.2 = (f32[3,2,32,256]{3,2,1,0:T(8,128)S(1)}, f32[3,2,32,256]{3,2,1,0:T(8,128)}, u32[]{:S(2)}) copy-start(f32[3,2,32,256]{3,2,1,0:T(8,128)} %param.13) | copy-start | bytes 589828
  54.7 27.3 %collective-permute-start.5 = (f32[3,2,1,128]{3,1,0,2:T(2,128)S(1)}, f32[3,2,1,128]{3,1,0,2:T(2,128)S(1)}, u32[]{:S(2)}, u32[]{:S(2)}) collective-permute-start(f32[3,2,1,128]{3,1,0,2:T(2,128)S(1)} %bitcast.608), channel_id=1, source_target_pairs={{0,1},{1,2},{2,3},{3,4},{4,5},{5,6},{6,7},{7,0},{8,9},{9,10},{10,1... | collective-permute-start | bytes 9224 | tf_op jit(solution)/shard_map/ppermute | solution.py:23
  56.8 38.4 %collective-permute-start.3 = (f32[3,2,2,16,128]{4,3,0,2,1:T(8,128)S(1)}, f32[3,2,2,16,128]{4,3,0,2,1:T(8,128)S(1)}, u32[]{:S(2)}, u32[]{:S(2)}) collective-permute-start(f32[3,2,2,16,128]{4,3,0,2,1:T(8,128)S(1)} %get-tuple-element.47), channel_id=1, source_target_pairs={{0,8},{8,16},{16,24},{24,32},{32,40},{40,48},{48,56},{56,64},{64,7... | collective-permute-start | bytes 294920 | tf_op jit(solution)/shard_map/ppermute | solution.py:23
  82.1 12.9 %collective-permute-start.6 = (f32[3,2,17,128]{3,2,0,1:T(8,128)S(1)}, f32[3,2,17,128]{3,2,0,1:T(8,128)S(1)}, u32[]{:S(2)}, u32[]{:S(2)}) collective-permute-start(f32[3,2,17,128]{3,2,0,1:T(8,128)S(1)} %get-tuple-element.92), channel_id=1, source_target_pairs={{0,504},{8,0},{16,8},{24,16},{32,24},{40,32},{48,40},{56,48},{64,5... | collective-permute-start | bytes 156680 | tf_op jit(solution)/shard_map/ppermute | solution.py:23
  95.2 7.0 %collective-permute-start.2 = (f32[3,2,2,128]{3,2,1,0:T(2,128)S(1)}, f32[3,2,2,128]{3,2,1,0:T(2,128)S(1)}, u32[]{:S(2)}, u32[]{:S(2)}) collective-permute-start(f32[3,2,2,128]{3,2,1,0:T(2,128)S(1)} %bitcast.604), channel_id=1, source_target_pairs={{0,1},{1,2},{2,3},{3,4},{4,5},{5,6},{6,7},{7,0},{8,9},{9,10},{10,1... | collective-permute-start | bytes 18440 | tf_op jit(solution)/shard_map/ppermute | solution.py:23
  100.0 3.1 %collective-permute-start.4 = (f32[3,2,2,128]{3,2,1,0:T(2,128)S(1)}, f32[3,2,2,128]{3,2,1,0:T(2,128)S(1)}, u32[]{:S(2)}, u32[]{:S(2)}) collective-permute-start(f32[3,2,2,128]{3,2,1,0:T(2,128)S(1)} %bitcast.602), channel_id=1, source_target_pairs={{0,1},{1,2},{2,3},{3,4},{4,5},{5,6},{6,7},{7,0},{8,9},{9,10},{10,1... | collective-permute-start | bytes 18440 | tf_op jit(solution)/shard_map/ppermute | solution.py:23
  108.2 13.7 %collective-permute-start.7 = (f32[3,2,16,128]{3,2,0,1:T(8,128)S(1)}, f32[3,2,16,128]{3,2,0,1:T(8,128)S(1)}, u32[]{:S(2)}, u32[]{:S(2)}) collective-permute-start(f32[3,2,16,128]{3,2,0,1:T(8,128)S(1)} %bitcast.543), channel_id=1, source_target_pairs={{0,504},{8,0},{16,8},{24,16},{32,24},{40,32},{48,40},{56,48},{64,5... | collective-permute-start | bytes 147464 | tf_op jit(solution)/shard_map/ppermute | solution.py:23
where the time goes:
time: 143 us; the launch traced here: 142 us
  local copies, waits for them, and re-layouts  80.6 us (56%)
  starting transfers between devices  50.1 us (35%)
  matrix products  5.96 us (4%)
  waiting for transfers between devices  2.5 us (2%)
  other arithmetic  2.12 us (1%)
    ppermute x8, starting transfers between devices, shifted(): lax.ppermute(x, axis, [(i, (i + by) % devices) for i in range(devices)])  50.1 us
    reshape x4, local copies, waits for them, and re-layouts, split_parity(): array.reshape(leading + (size_x // 2, 2, size_y // 2, 2, size_z // 2, 2))  43.1 us
    reshape x1, local copies, waits for them, and re-layouts, merge_parity(): return moved.reshape((shape[0], shape[4] * 2, shape[5] * 2, shape[6] * 2))  10.3 us
    broadcast_in_dim x2, local copies, waits for them, and re-layouts, on_device(): jnp.where(element_phase[None] == phase_ids[:, None, None, None], element_...  9.17 us
    eq x2, local copies, waits for them, and re-layouts, on_device(): element_phase[None] == phase_ids[:, None, None, None]  8.4 us
    transpose x1, local copies, waits for them, and re-layouts, merge_parity(): moved = parted.transpose((0, 4, 1, 5, 2, 6, 3))  6.73 us
    dot_general x2, matrix products, split_update(): coupled = jnp.tensordot(off_table, wflat, axes=1, precision=highest)  4.72 us
  transfers between devices with their start and end apart: 8, of which 3 were waited for; matrix products, arithmetic and copies ran while one was open for 33% of the time, Pallas kernels for 0%

commit v1 on v0

v1 whole, which is shorter than its diff:
```python
import jax
import jax.numpy as jnp
from jax import lax
from jax.experimental import pallas as pl
from jax.experimental.pallas import tpu as pltpu
from jax.sharding import PartitionSpec as P

PARITY = {"0": (0, 0), "1": (1, 1), "s": (0, 1), "o": (1, 0)}


def shifted(x, axis, by):
    devices = lax.axis_size(axis)
    return lax.ppermute(x, axis, [(i, (i + by) % devices) for i in range(devices)])


def tiles(a):
    rows, cols = a.shape
    return jnp.stack(
        [a[r : r + 8, c : c + 128] for r in range(0, rows, 8) for c in range(0, cols, 128)]
    )


def flat(t, cols):
    across = cols // 128
    rows = [
        jnp.concatenate([t[r + c] for c in range(across)], axis=1)
        for r in range(0, t.shape[0], across)
    ]
    return jnp.concatenate(rows, axis=0)


def even_lanes(shape):
    return lax.broadcasted_iota(jnp.int32, shape, len(shape) - 1) % 2 == 0


def next_lane(a):
    return pltpu.roll(a, a.shape[-1] - 1, a.ndim - 1)


def last_lane(a):
    return pltpu.roll(a, 1, a.ndim - 1)


def down_row(a, top):
    first = lax.broadcasted_iota(jnp.int32, a.shape, 0) == 0
    return jnp.where(first, jnp.broadcast_to(top, a.shape), pltpu.roll(a, 1, 0))


def pair_even(a):
    here, there = tiles(a), tiles(next_lane(a))
    even = even_lanes((8, 128))[None]
    return {"s": jnp.where(even, here, there), "o": jnp.where(even, there, here)}


def pair_odd(a):
    return {"0": tiles(a), "1": tiles(next_lane(a))}


def plane_views(even_rows, odd_rows, tops):
    same = [pair_even(a) for a in even_rows]
    after = [pair_odd(a) for a in odd_rows]
    before = [pair_odd(down_row(a, top)) for a, top in zip(odd_rows, tops)]
    return same, after, before


class Elements:
    def __init__(self, modulus, phase):
        self.modulus = tiles(modulus)
        self.phase = tiles(phase)


class Summer:
    def __init__(self, table):
        self.table = table
        self.even = even_lanes((8, 128))
        self.corners = 8

    def entry(self, elements, corner, partner, kind, i, j):
        first, second = PARITY[kind]
        picked = []
        for ph in range(3):
            places = []
            for parity, side in ((0, first), (1, second)):
                c = corner * 2 + parity
                d = partner * 2 + side
                places.append(self.table[(((ph * 8 + c) * 8 + d) * 3 + i) * 3 + j])
            picked.append(jnp.where(self.even, places[0], places[1])[None])
        return jnp.where(
            elements.phase == 0, picked[0], jnp.where(elements.phase == 1, picked[1], picked[2])
        )

    def force(self, elements, corner, terms):
        total = [None] * 3
        for partner, kind, values in terms:
            for i in range(3):
                for j in range(3):
                    part = self.entry(elements, corner, partner, kind, i, j) * values[j]
                    total[i] = part if total[i] is None else total[i] + part
        return [elements.modulus * part for part in total]

    def diagonal(self, elements, corner):
        return [
            elements.modulus * self.entry(elements, corner, corner, "s", i, j)
            for i in range(3)
            for j in range(3)
        ]


def pick(views, kind):
    return [view[kind] for view in views]


def terms_of(views, cx, cy, dx, kinds):
    same, after, before = views
    other = after if cy == 0 else before
    found = [(dx * 2 + cy, kind, pick(same, kind)) for kind in kinds]
    found += [(dx * 2 + 1 - cy, kind, pick(other, kind)) for kind in ("0", "1")]
    return found


def added(left, right):
    return [a + b for a, b in zip(left, right)]


def at_nodes(parts, cols):
    out = []
    for part in parts:
        whole = flat(part, cols)
        out.append(whole + last_lane(whole))
    return out


def inverse_of(m):
    m00, m01, m02, m10, m11, m12, m20, m21, m22 = m
    c00 = m11 * m22 - m12 * m21
    c01 = m12 * m20 - m10 * m22
    c02 = m10 * m21 - m11 * m20
    c10 = m02 * m21 - m01 * m22
    c11 = m00 * m22 - m02 * m20
    c12 = m01 * m20 - m00 * m21
    c20 = m01 * m12 - m02 * m11
    c21 = m02 * m10 - m00 * m12
    c22 = m00 * m11 - m01 * m10
    determinant = m00 * c00 + m01 * c01 + m02 * c02
    scale = 1.0 / determinant
    return [a * scale for a in (c00, c10, c20, c01, c11, c21, c02, c12, c22)]


def applied(inverse, right):
    return [sum(inverse[3 * i + j] * right[j] for j in range(3)) for i in range(3)]


class Rows:
    def __init__(self, work_ref):
        self.work, self.slot = work_ref, 0

    def split(self, a):
        parts, slot, half = a.shape[1] // 128, self.slot, a.shape[0] // 2
        self.slot += 1
        for k in range(parts):
            self.work[slot, k] = a[:, k * 128 : (k + 1) * 128]
        return tuple(
            jnp.concatenate([self.work[slot, k, pl.ds(bit, half, 2), :] for k in range(parts)], axis=1)
            for bit in range(2)
        )

    def merge(self, even, odd):
        parts, slot, half = even.shape[1] // 128, self.slot, even.shape[0]
        self.slot += 1
        for k in range(parts):
            self.work[slot, k, pl.ds(0, half, 2), :] = even[:, k * 128 : (k + 1) * 128]
            self.work[slot, k, pl.ds(1, half, 2), :] = odd[:, k * 128 : (k + 1) * 128]
        return jnp.concatenate([self.work[slot, k] for k in range(parts)], axis=1)


def local_plane(rows, u_ref, halo_ref, plane):
    split = [rows.split(u_ref[c, plane]) for c in range(3)]
    even, odd = [a for a, _ in split], [b for _, b in split]
    tops = [halo_ref[3 * plane + c : 3 * plane + c + 1, :] for c in range(3)]
    return even, odd, tops


def element_rows(rows, mod_ref, phase_ref, halo_ref, plane):
    split = [rows.split(mod_ref[plane]), rows.split(phase_ref[plane].astype(jnp.float32))]
    even, odd = [a for a, _ in split], [b for _, b in split]
    before = (
        down_row(odd[0], halo_ref[6 + plane : 7 + plane, :]),
        down_row(odd[1], halo_ref[8 + plane : 9 + plane, :]),
    )
    return even, before


def rim_kernel(u_ref, mod_ref, phase_ref, out_ref):
    out_ref[...] = jnp.zeros(out_ref.shape, jnp.float32)
    for plane in range(2):
        for c in range(3):
            out_ref[3 * plane + c : 3 * plane + c + 1, :] = u_ref[c, plane, 7:8, :]
        out_ref[6 + plane : 7 + plane, :] = mod_ref[plane, 7:8, :]
        out_ref[8 + plane : 9 + plane, :] = phase_ref[plane, 7:8, :].astype(jnp.float32)


def pack_kernel(table, u_ref, load_ref, mod_ref, phase_ref, halo_ref, back_ref, ahead_ref, work_ref):
    half, cols = u_ref.shape[2] // 2, u_ref.shape[3]
    quarter = half // 2
    summer, rows = Summer(table), Rows(work_ref)
    even_zero, odd_zero, top_zero = local_plane(rows, u_ref, halo_ref, 0)
    even_one, odd_one, top_one = local_plane(rows, u_ref, halo_ref, 1)
    zero = plane_views(even_zero, odd_zero, top_zero)
    one = plane_views(even_one, odd_one, top_one)
    rows_zero = element_rows(rows, mod_ref, phase_ref, halo_ref, 0)
    rows_one = element_rows(rows, mod_ref, phase_ref, halo_ref, 1)
    even = even_lanes((half, cols))
    own, beyond = None, None
    for cy in range(2):
        elements = Elements(*rows_zero[cy])
        part = summer.force(
            elements, cy, terms_of(zero, 0, cy, 0, "o") + terms_of(one, 0, cy, 1, "so")
        )
        own = part if own is None else added(own, part)
        elements = Elements(*rows_one[cy])
        part = summer.force(elements, 2 + cy, terms_of(one, 1, cy, 0, "so"))
        beyond = part if beyond is None else added(beyond, part)
    own = at_nodes(own, cols)
    beyond = at_nodes(beyond, cols)
    back_ref[160:168, :] = jnp.zeros((8, cols), jnp.float32)
    for c in range(3):
        left = rows.split(load_ref[c, 0])[0] - own[c]
        back_ref[c * half : (c + 1) * half, :] = jnp.where(even, left, even_zero[c])
        back_ref[(3 + c) * half : (4 + c) * half, :] = odd_zero[c]
        back_ref[10 * half + c : 10 * half + c + 1, :] = top_zero[c]
    for cy in range(2):
        for k in range(2):
            back_ref[(6 + 2 * k + cy) * half : (7 + 2 * k + cy) * half, :] = rows_zero[cy][k]
            start = half + quarter + (2 * k + cy) * half
            ahead_ref[start : start + half, :] = rows_one[cy][k]
    ahead_ref[0:half, :] = jnp.where(even, beyond[0], last_lane(beyond[1]))
    ahead_ref[half : half + quarter, :] = jnp.where(
        even[:quarter], beyond[2][:quarter], last_lane(beyond[2][quarter:])
    )


def inner_kernel(table, u_ref, load_ref, mod_ref, phase_ref, halo_ref, sums_ref, work_ref):
    half, cols = u_ref.shape[2] // 2, u_ref.shape[3]
    summer, rows = Summer(table), Rows(work_ref)
    zero = plane_views(*local_plane(rows, u_ref, halo_ref, 0))
    one = plane_views(*local_plane(rows, u_ref, halo_ref, 1))
    rows_zero = element_rows(rows, mod_ref, phase_ref, halo_ref, 0)
    rows_one = element_rows(rows, mod_ref, phase_ref, halo_ref, 1)
    total, middle, first, last = None, None, None, None
    for cy in range(2):
        left, right = Elements(*rows_zero[cy]), Elements(*rows_one[cy])
        part = summer.force(left, 2 + cy, terms_of(zero, 1, cy, 0, "o") + terms_of(one, 1, cy, 1, "o"))
        part = added(part, summer.force(right, cy, terms_of(one, 0, cy, 0, "o")))
        total = part if total is None else added(total, part)
        near = summer.diagonal(left, cy)
        mid = added(summer.diagonal(left, 2 + cy), summer.diagonal(right, cy))
        far = summer.diagonal(right, 2 + cy)
        first = near if first is None else added(first, near)
        middle = mid if middle is None else added(middle, mid)
        last = far if last is None else added(last, far)
    total = at_nodes(total, cols)
    for c in range(3):
        sums_ref[c] = rows.split(load_ref[c, 1])[0] - total[c]
    solved = inverse_of(at_nodes(middle, cols))
    first = at_nodes(first, cols)
    last = at_nodes(last, cols)
    for k in range(9):
        sums_ref[3 + k] = solved[k]
        sums_ref[12 + k] = first[k]
        sums_ref[21 + k] = last[k]


def unpacked(ref, half):
    quarter = half // 2
    block = ref[0:half, :]
    rest = ref[half : half + quarter, :]
    return [block, next_lane(block), jnp.concatenate([rest, next_lane(rest)], axis=0)]


def finish_kernel(
    table, u_ref, mod_ref, phase_ref, halo_ref, sums_ref, mine_back, mine_ahead, back_ref, ahead_ref, out_ref, work_ref
):
    half, cols = u_ref.shape[2] // 2, u_ref.shape[3]
    quarter = half // 2
    summer, rows = Summer(table), Rows(work_ref)
    even_zero, odd_zero, top_zero = local_plane(rows, u_ref, halo_ref, 0)
    zero = plane_views(even_zero, odd_zero, top_zero)
    rows_zero = element_rows(rows, mod_ref, phase_ref, halo_ref, 0)
    rows_one = element_rows(rows, mod_ref, phase_ref, halo_ref, 1)
    even_two = [back_ref[c * half : (c + 1) * half, :] for c in range(3)]
    odd_two = [back_ref[(3 + c) * half : (4 + c) * half, :] for c in range(3)]
    top_two = [back_ref[10 * half + c : 10 * half + c + 1, :] for c in range(3)]
    two = plane_views(even_two, odd_two, top_two)
    even = even_lanes((half, cols))
    before, after, lower, upper, beyond = None, None, None, None, None
    for cy in range(2):
        start = half + quarter + cy * half
        minus = Elements(ahead_ref[start : start + half, :], ahead_ref[start + 2 * half : start + 3 * half, :])
        start = (6 + cy) * half
        plus = Elements(back_ref[start : start + half, :], back_ref[start + 2 * half : start + 3 * half, :])
        right = Elements(*rows_one[cy])
        part = summer.force(minus, 2 + cy, terms_of(zero, 1, cy, 1, "o"))
        before = part if before is None else added(before, part)
        part = summer.force(right, 2 + cy, terms_of(two, 1, cy, 1, "o"))
        after = part if after is None else added(after, part)
        part = summer.force(right, cy, terms_of(two, 0, cy, 1, "o"))
        beyond = part if beyond is None else added(beyond, part)
        part = summer.diagonal(minus, 2 + cy)
        lower = part if lower is None else added(lower, part)
        part = summer.diagonal(plus, cy)
        upper = part if upper is None else added(upper, part)
    before, after = at_nodes(before, cols), at_nodes(after, cols)
    lower, upper = at_nodes(lower, cols), at_nodes(upper, cols)
    came, sent = unpacked(ahead_ref, half), unpacked(mine_ahead, half)
    right = [mine_back[c * half : (c + 1) * half, :] - came[c] - before[c] for c in range(3)]
    first_new = applied(inverse_of([sums_ref[12 + k] + lower[k] for k in range(9)]), right)
    right = [even_two[c] - sent[c] - after[c] for c in range(3)]
    third_new = applied(inverse_of([sums_ref[21 + k] + upper[k] for k in range(9)]), right)
    near = [pair_even(a)["s"] for a in first_new]
    far = [pair_even(a)["s"] for a in third_new]
    for cy in range(2):
        left, right = Elements(*rows_zero[cy]), Elements(*rows_one[cy])
        beyond = added(beyond, summer.force(left, 2 + cy, [(cy, "s", near)]))
        beyond = added(beyond, summer.force(right, cy, [(2 + cy, "s", far)]))
    beyond = at_nodes(beyond, cols)
    solved = [sums_ref[3 + k] for k in range(9)]
    second_new = applied(solved, [sums_ref[c] - beyond[c] for c in range(3)])
    for c in range(3):
        out_ref[c, 0] = rows.merge(jnp.where(even, first_new[c], even_zero[c]), odd_zero[c])
        own, other = rows.split(u_ref[c, 1])
        out_ref[c, 1] = rows.merge(jnp.where(even, second_new[c], own), other)


def whole():
    return pl.BlockSpec(memory_space=pltpu.VMEM)


def scalars():
    return pl.BlockSpec(memory_space=pltpu.SMEM)


def on_device(displacement, load, element_phase, element_modulus, stiffness):
    planes, rows, cols = displacement.shape[1:]
    half = rows // 2
    kind = displacement.dtype
    table = stiffness.reshape(-1)
    last = rows // 8 - 1
    slots = 16
    rim = pl.pallas_call(
        rim_kernel,
        grid=(1,),
        in_specs=[
            pl.BlockSpec((3, planes, 8, cols), lambda i: (0, 0, last, 0)),
            pl.BlockSpec((planes, 8, cols), lambda i: (0, last, 0)),
            pl.BlockSpec((planes, 8, cols), lambda i: (0, last, 0)),
        ],
        out_specs=pl.BlockSpec((16, cols), lambda i: (0, 0)),
        out_shape=jax.ShapeDtypeStruct((16, cols), kind),
    )(displacement, element_modulus, element_phase)
    halo = shifted(rim, "gy", 1)
    back_rows, ahead_rows = 10 * half + 8, 5 * half + half // 2
    back, ahead = pl.pallas_call(
        pack_kernel,
        in_specs=[scalars()] + [whole()] * 5,
        out_specs=[whole()] * 2,
        out_shape=[
            jax.ShapeDtypeStruct((back_rows, cols), kind),
            jax.ShapeDtypeStruct((ahead_rows, cols), kind),
        ],
        scratch_shapes=[pltpu.VMEM((slots, cols // 128, rows, 128), kind)],
        compiler_params=pltpu.CompilerParams(vmem_limit_bytes=24 << 20),
    )(table, displacement, load, element_modulus, element_phase, halo)
    from_next = shifted(back, "gx", -1)
    from_last = shifted(ahead, "gx", 1)
    sums = pl.pallas_call(
        inner_kernel,
        in_specs=[scalars()] + [whole()] * 5,
        out_specs=whole(),
        out_shape=jax.ShapeDtypeStruct((30, half, cols), kind),
        scratch_shapes=[pltpu.VMEM((slots, cols // 128, rows, 128), kind)],
        compiler_params=pltpu.CompilerParams(vmem_limit_bytes=24 << 20),
        cost_estimate=pl.CostEstimate(flops=20_000_000, bytes_accessed=1_000_000, transcendentals=0),
    )(table, displacement, load, element_modulus, element_phase, halo)
    return pl.pallas_call(
        finish_kernel,
        in_specs=[scalars()] + [whole()] * 9,
        out_specs=whole(),
        out_shape=jax.ShapeDtypeStruct(displacement.shape, kind),
        scratch_shapes=[pltpu.VMEM((slots, cols // 128, rows, 128), kind)],
        compiler_params=pltpu.CompilerParams(vmem_limit_bytes=24 << 20),
    )(
        table, displacement, element_modulus, element_phase, halo, sums, back, ahead, from_next, from_last
    )


def solution(mesh):
    in_specs = (
        P(None, "gx", "gy", None),
        P(None, "gx", "gy", None),
        P("gx", "gy", None),
        P("gx", "gy", None),
        P(),
    )
    out_specs = P(None, "gx", "gy", None)
    return jax.shard_map(
        on_device, mesh=mesh, in_specs=in_specs, out_specs=out_specs, check_vma=False
    )
```

time: 143 us -> 41.8 us (0.29)
  local copies, waits for them, and re-layouts: 80.6 us -> 0.77 us
  starting transfers between devices: 50.1 us -> 19.3 us
  waiting for transfers between devices: 2.5 us -> 14.3 us
  Pallas kernels: 0 us -> 7.18 us
  matrix products: 5.96 us -> 0 us
  other arithmetic: 2.12 us -> 0 us
    reshape x5 -> x1, local copies, waits for them, and re-layouts: 53.4 us -> 0.25 us  [on_device(): table = stiffness.reshape(-1)]
    ppermute x8 -> x3, starting transfers between devices: 50.1 us -> 19.3 us  [shifted(): lax.ppermute(x, axis, [(i, (i + by) % devices) for i in range(devices)])]
    ppermute x8 -> x3, waiting for transfers between devices: 2.5 us -> 14.3 us  [shifted(): lax.ppermute(x, axis, [(i, (i + by) % devices) for i in range(devices)])]
    broadcast_in_dim x6 -> x0, local copies, waits for them, and re-layouts: 9.21 us -> none  [the longest x2 9.17 us: on_device(): jnp.where(element_phase[None] == phase_ids[:, None, None, None], element_...]
    eq x2 -> x0, local copies, waits for them, and re-layouts: 8.4 us -> none  [on_device(): element_phase[None] == phase_ids[:, None, None, None]]
    pallas_call x0 -> x4, Pallas kernels: none -> 7.18 us  [the longest x1 2.48 us: on_device(): pl.pallas_call(finish_kernel, in_specs=[scalars()] + [whole()] * 9, out_s...]
    transpose x1 -> x0, local copies, waits for them, and re-layouts: 6.73 us -> none  [merge_parity(): moved = parted.transpose((0, 4, 1, 5, 2, 6, 3))]
    dot_general x5 -> x0, matrix products: 5.96 us -> none  [the longest x2 4.72 us: split_update(): coupled = jnp.tensordot(off_table, wflat, axes=1, precision=highest)]
  transfers between devices with their start and end apart: 8 -> 3, of which waited for: 3 -> 2; matrix products, arithmetic and copies ran while one was open for 33% -> 2% of each run, Pallas kernels for 0% -> 4%
where the time goes in v1:
time: 41.8 us; the launch traced here: 41.6 us
  starting transfers between devices  19.3 us (46%)
  waiting for transfers between devices  14.3 us (34%)
  Pallas kernels  7.18 us (17%)
  local copies, waits for them, and re-layouts  0.77 us (2%)
    ppermute x3, starting transfers between devices, shifted(): lax.ppermute(x, axis, [(i, (i + by) % devices) for i in range(devices)])  19.3 us
    ppermute x3, waiting for transfers between devices, shifted(): lax.ppermute(x, axis, [(i, (i + by) % devices) for i in range(devices)])  14.3 us
    pallas_call x1, Pallas kernels, on_device(): pl.pallas_call(finish_kernel, in_specs=[scalars()] + [whole()] * 9, out_s...  2.48 us
    pallas_call x1, Pallas kernels, on_device(): pl.pallas_call(inner_kernel, in_specs=[scalars()] + [whole()] * 5, out_sp...  1.63 us
    pallas_call x1, Pallas kernels, on_device(): pl.pallas_call(pack_kernel, in_specs=[scalars()] + [whole()] * 5, out_spe...  1.6 us
    pallas_call x1, Pallas kernels, on_device(): pl.pallas_call(rim_kernel, grid=(1,), in_specs=[pl.BlockSpec((3, planes,...  1.46 us
  transfers between devices with their start and end apart: 3, of which 2 were waited for; matrix products, arithmetic and copies ran while one was open for 2% of the time, Pallas kernels for 4%

profile of v1, /device:TPU:1, one launch (start us, length us, event | category | flops | bytes accessed | tf_op | source)
XLA Modules:
  0.0 41.6 jit_solution(11863093186022926425)
XLA Ops:
  0.0 0.0 copy-start.4
  0.0 1.5 %shard_map.55 = f32[16,256]{1,0:T(8,128)} custom-call(f32[3,2,32,256]{3,2,1,0:T(8,128)} %u_ref.7, f32[2,32,256]{2,1,0:T(8,128)} %mod_ref.7, s32[2,32,256]{2,1,0:T(8,128)} %phase_ref.7), custom_call_target="tpu_custom_call" | custom-call | tf_op jit(solution)/shard_map/pallas_call | solution.py:349
  1.5 5.4 %collective-permute-start = (f32[16,256]{1,0:T(8,128)}, f32[16,256]{1,0:T(8,128)S(1)}, u32[]{:S(2)}, u32[]{:S(2)}) collective-permute-start(f32[16,256]{1,0:T(8,128)} %shard_map.55), channel_id=1, source_target_pairs={{0,1},{1,2},{2,3},{3,4},{4,5},{5,6},{6,7},{7,0},{8,9},{9,10},{10,1... | collective-permute-start | bytes 49160 | tf_op jit(solution)/shard_map/ppermute | solution.py:13
  6.9 0.0 copy-done.4
  6.9 0.0 copy-start.3
  6.9 0.5 %copy.6 = f32[3,8,8,3,3]{4,3,2,1,0:T(4,128)S(1)} copy(f32[3,8,8,3,3]{2,1,4,3,0:T(8,128)S(1)} %copy-done.4) | data formatting | bytes 13824 | tf_op args[4]
  7.4 0.0 copy-start
  7.4 0.0 copy-start.1
  7.4 0.0 copy-start.2
  7.4 0.3 reshape.3.table
  7.6 3.5 %collective-permute-done.halo_ref = f32[16,256]{1,0:T(8,128)S(1)} collective-permute-done((f32[16,256]{1,0:T(8,128)}, f32[16,256]{1,0:T(8,128)S(1)}, u32[]{:S(2)}, u32[]{:S(2)}) %collective-permute-start) | collective-permute-done | bytes 16416 | tf_op jit(solution)/shard_map/ppermute | solution.py:13
  11.1 0.0 copy-done.3
  11.1 0.0 copy-done
  11.1 0.0 copy-done.1
  11.1 0.0 copy-done.2
  11.1 1.6 %shard_map.57 = (f32[168,256]{1,0:T(8,128)S(1)}, f32[88,256]{1,0:T(8,128)S(1)}) custom-call(f32[1728]{0:T(1024)S(1)} %reshape.3.table, f32[3,2,32,256]{3,2,1,0:T(8,128)S(1)} %copy-done, f32[3,2,32,256]{3,2,1,0:T(8,128)S(1)} %copy-done.3, f32[2,32,256]{2,1,0:T(8,128)S(1)} %copy-done.1, s32[2,32,256]{2,1,0:T(8,128)S(1)} %copy-done.2, ...), custom_call_target="tpu_custom_call" | custom-call | tf_op jit(solution)/shard_map/pallas_call | solution.py:362
  12.8 12.1 %collective-permute-start.1 = (f32[168,256]{1,0:T(8,128)S(1)}, f32[168,256]{1,0:T(8,128)S(1)}, u32[]{:S(2)}, u32[]{:S(2)}) collective-permute-start(f32[168,256]{1,0:T(8,128)S(1)} %get-tuple-element.7.mine_back), channel_id=1, source_target_pairs={{0,504},{8,0},{16,8},{24,16},{32,24},{40,32},{48,40},{56,48},{64,5... | collective-permute-start | bytes 516104 | tf_op jit(solution)/shard_map/ppermute | solution.py:13
  24.8 1.9 %collective-permute-start.2 = (f32[88,256]{1,0:T(8,128)S(1)}, f32[88,256]{1,0:T(8,128)S(1)}, u32[]{:S(2)}, u32[]{:S(2)}) collective-permute-start(f32[88,256]{1,0:T(8,128)S(1)} %get-tuple-element.8.mine_ahead), channel_id=1, source_target_pairs={{0,8},{8,16},{16,24},{24,32},{32,40},{40,48},{48,56},{56,64},{64,7... | collective-permute-start | bytes 270344 | tf_op jit(solution)/shard_map/ppermute | solution.py:13
  26.7 1.6 %shard_map.56.sums_ref = f32[30,16,256]{2,1,0:T(8,128)S(1)} custom-call(f32[1728]{0:T(1024)S(1)} %reshape.3.table, f32[3,2,32,256]{3,2,1,0:T(8,128)S(1)} %copy-done, f32[3,2,32,256]{3,2,1,0:T(8,128)S(1)} %copy-done.3, f32[2,32,256]{2,1,0:T(8,128)S(1)} %copy-done.1, s32[2,32,256]{2,1,0:T(8,128)S(1)} %copy-done.2, f32[16,256]{1,0:T(8,128)S(1)} %collective-permute-done.halo_ref), custom_call_target="tpu_custom_call" | custom-call | flops 20000000 | bytes 1000000 | tf_op jit(solution)/shard_map/pallas_call | solution.py:375
  28.4 10.8 %collective-permute-done.2.ahead_ref = f32[88,256]{1,0:T(8,128)S(1)} collective-permute-done((f32[88,256]{1,0:T(8,128)S(1)}, f32[88,256]{1,0:T(8,128)S(1)}, u32[]{:S(2)}, u32[]{:S(2)}) %collective-permute-start.2) | collective-permute-done | bytes 90144 | tf_op jit(solution)/shard_map/ppermute | solution.py:13
  39.2 0.0 collective-permute-done.1.back_ref
  39.2 2.5 %shard_map.58 = f32[3,2,32,256]{3,2,1,0:T(8,128)} custom-call(f32[1728]{0:T(1024)S(1)} %reshape.3.table, f32[3,2,32,256]{3,2,1,0:T(8,128)S(1)} %copy-done, f32[2,32,256]{2,1,0:T(8,128)S(1)} %copy-done.1, s32[2,32,256]{2,1,0:T(8,128)S(1)} %copy-done.2, f32[16,256]{1,0:T(8,128)S(1)} %collective-permute-done.halo_ref, f32[30,16,256]{2,1,0:T(8,128)S(1)} %shard_map.56.sums_ref, ...), custom_call_target="tpu_custom_call" | custom-call | tf_op jit(solution)/shard_map/pallas_call | solution.py:384
Async XLA Ops:
  0.0 6.9 %copy-start.4 = (f32[3,8,8,3,3]{2,1,4,3,0:T(8,128)S(1)}, f32[3,8,8,3,3]{2,1,4,3,0:T(8,128)}, u32[]{:S(2)}) copy-start(f32[3,8,8,3,3]{2,1,4,3,0:T(8,128)} %param.9) | copy-start | bytes 20740
  1.5 9.7 %collective-permute-start = (f32[16,256]{1,0:T(8,128)}, f32[16,256]{1,0:T(8,128)S(1)}, u32[]{:S(2)}, u32[]{:S(2)}) collective-permute-start(f32[16,256]{1,0:T(8,128)} %shard_map.55), channel_id=1, source_target_pairs={{0,1},{1,2},{2,3},{3,4},{4,5},{5,6},{6,7},{7,0},{8,9},{9,10},{10,1... | collective-permute-start | bytes 49160 | tf_op jit(solution)/shard_map/ppermute | solution.py:13
  6.9 4.3 %copy-start.3 = (f32[3,2,32,256]{3,2,1,0:T(8,128)S(1)}, f32[3,2,32,256]{3,2,1,0:T(8,128)}, u32[]{:S(2)}) copy-start(f32[3,2,32,256]{3,2,1,0:T(8,128)} %load_ref.3) | copy-start | bytes 589828
  7.4 3.8 %copy-start = (f32[3,2,32,256]{3,2,1,0:T(8,128)S(1)}, f32[3,2,32,256]{3,2,1,0:T(8,128)}, u32[]{:S(2)}) copy-start(f32[3,2,32,256]{3,2,1,0:T(8,128)} %u_ref.7) | copy-start | bytes 589828
  7.4 3.8 %copy-start.1 = (f32[2,32,256]{2,1,0:T(8,128)S(1)}, f32[2,32,256]{2,1,0:T(8,128)}, u32[]{:S(2)}) copy-start(f32[2,32,256]{2,1,0:T(8,128)} %mod_ref.7) | copy-start | bytes 196612
  7.4 3.8 %copy-start.2 = (s32[2,32,256]{2,1,0:T(8,128)S(1)}, s32[2,32,256]{2,1,0:T(8,128)}, u32[]{:S(2)}) copy-start(s32[2,32,256]{2,1,0:T(8,128)} %phase_ref.7) | copy-start | bytes 196612
  12.8 26.4 %collective-permute-start.1 = (f32[168,256]{1,0:T(8,128)S(1)}, f32[168,256]{1,0:T(8,128)S(1)}, u32[]{:S(2)}, u32[]{:S(2)}) collective-permute-start(f32[168,256]{1,0:T(8,128)S(1)} %get-tuple-element.7.mine_back), channel_id=1, source_target_pairs={{0,504},{8,0},{16,8},{24,16},{32,24},{40,32},{48,40},{56,48},{64,5... | collective-permute-start | bytes 516104 | tf_op jit(solution)/shard_map/ppermute | solution.py:13
  24.8 14.3 %collective-permute-start.2 = (f32[88,256]{1,0:T(8,128)S(1)}, f32[88,256]{1,0:T(8,128)S(1)}, u32[]{:S(2)}, u32[]{:S(2)}) collective-permute-start(f32[88,256]{1,0:T(8,128)S(1)} %get-tuple-element.8.mine_ahead), channel_id=1, source_target_pairs={{0,8},{8,16},{16,24},{24,32},{32,40},{40,48},{48,56},{56,64},{64,7... | collective-permute-start | bytes 270344 | tf_op jit(solution)/shard_map/ppermute | solution.py:13

commit v2 on v1

--- a/solution.py
+++ b/solution.py
@@ -11,6 +11,11 @@
 def shifted(x, axis, by):
     devices = lax.axis_size(axis)
     return lax.ppermute(x, axis, [(i, (i + by) % devices) for i in range(devices)])
+
+
+def shifted_from(x, axis, by, parity):
+    devices = lax.axis_size(axis)
+    return lax.ppermute(x, axis, [(i, (i + by) % devices) for i in range(parity, devices, 2)])
 
 
 def tiles(a):
@@ -199,44 +204,54 @@
         out_ref[8 + plane : 9 + plane, :] = phase_ref[plane, 7:8, :].astype(jnp.float32)
 
 
-def pack_kernel(table, u_ref, load_ref, mod_ref, phase_ref, halo_ref, back_ref, ahead_ref, work_ref):
+def ahead_kernel(table, u_ref, mod_ref, phase_ref, halo_ref, back_ref, ahead_ref, top_ref, end_ref, work_ref):
     half, cols = u_ref.shape[2] // 2, u_ref.shape[3]
     quarter = half // 2
     summer, rows = Summer(table), Rows(work_ref)
-    even_zero, odd_zero, top_zero = local_plane(rows, u_ref, halo_ref, 0)
-    even_one, odd_one, top_one = local_plane(rows, u_ref, halo_ref, 1)
-    zero = plane_views(even_zero, odd_zero, top_zero)
-    one = plane_views(even_one, odd_one, top_one)
-    rows_zero = element_rows(rows, mod_ref, phase_ref, halo_ref, 0)
+    top_ref[...] = back_ref[: top_ref.shape[0], :]
+    end_ref[...] = back_ref[top_ref.shape[0] :, :]
+    one = plane_views(*local_plane(rows, u_ref, halo_ref, 1))
     rows_one = element_rows(rows, mod_ref, phase_ref, halo_ref, 1)
     even = even_lanes((half, cols))
-    own, beyond = None, None
+    beyond = None
+    for cy in range(2):
+        elements = Elements(*rows_one[cy])
+        part = summer.force(elements, 2 + cy, terms_of(one, 1, cy, 0, "so"))
+        beyond = part if beyond is None else added(beyond, part)
+        for k in range(2):
+            start = half + quarter + (2 * k + cy) * half
+            ahead_ref[start : start + half, :] = rows_one[cy][k]
+    beyond = at_nodes(beyond, cols)
+    ahead_ref[0:half, :] = jnp.where(even, beyond[0], last_lane(beyond[1]))
+    ahead_ref[half : half + quarter, :] = jnp.where(
+        even[:quarter], beyond[2][:quarter], last_lane(beyond[2][quarter:])
+    )
+
+
+def back_kernel(table, u_ref, load_ref, mod_ref, phase_ref, halo_ref, back_ref, work_ref):
+    half, cols = u_ref.shape[2] // 2, u_ref.shape[3]
+    summer, rows = Summer(table), Rows(work_ref)
+    even_zero, odd_zero, top_zero = local_plane(rows, u_ref, halo_ref, 0)
+    zero = plane_views(even_zero, odd_zero, top_zero)
+    one = plane_views(*local_plane(rows, u_ref, halo_ref, 1))
+    rows_zero = element_rows(rows, mod_ref, phase_ref, halo_ref, 0)
+    even = even_lanes((half, cols))
+    own = None
     for cy in range(2):
         elements = Elements(*rows_zero[cy])
         part = summer.force(
             elements, cy, terms_of(zero, 0, cy, 0, "o") + terms_of(one, 0, cy, 1, "so")
         )
         own = part if own is None else added(own, part)
-        elements = Elements(*rows_one[cy])
-        part = summer.force(elements, 2 + cy, terms_of(one, 1, cy, 0, "so"))
-        beyond = part if beyond is None else added(beyond, part)
+        for k in range(2):
+            back_ref[(6 + 2 * k + cy) * half : (7 + 2 * k + cy) * half, :] = rows_zero[cy][k]
     own = at_nodes(own, cols)
-    beyond = at_nodes(beyond, cols)
-    back_ref[160:168, :] = jnp.zeros((8, cols), jnp.float32)
+    back_ref[10 * half :, :] = jnp.zeros((8, cols), jnp.float32)
     for c in range(3):
         left = rows.split(load_ref[c, 0])[0] - own[c]
         back_ref[c * half : (c + 1) * half, :] = jnp.where(even, left, even_zero[c])
         back_ref[(3 + c) * half : (4 + c) * half, :] = odd_zero[c]
         back_ref[10 * half + c : 10 * half + c + 1, :] = top_zero[c]
-    for cy in range(2):
-        for k in range(2):
-            back_ref[(6 + 2 * k + cy) * half : (7 + 2 * k + cy) * half, :] = rows_zero[cy][k]
-            start = half + quarter + (2 * k + cy) * half
-            ahead_ref[start : start + half, :] = rows_one[cy][k]
-    ahead_ref[0:half, :] = jnp.where(even, beyond[0], last_lane(beyond[1]))
-    ahead_ref[half : half + quarter, :] = jnp.where(
-        even[:quarter], beyond[2][:quarter], last_lane(beyond[2][quarter:])
-    )
 
 
 def inner_kernel(table, u_ref, load_ref, mod_ref, phase_ref, halo_ref, sums_ref, work_ref):
@@ -270,18 +285,19 @@
         sums_ref[21 + k] = last[k]
 
 
-def unpacked(ref, half):
+def unpacked(a, half):
     quarter = half // 2
-    block = ref[0:half, :]
-    rest = ref[half : half + quarter, :]
+    block = a[0:half, :]
+    rest = a[half : half + quarter, :]
     return [block, next_lane(block), jnp.concatenate([rest, next_lane(rest)], axis=0)]
 
 
 def finish_kernel(
-    table, u_ref, mod_ref, phase_ref, halo_ref, sums_ref, mine_back, mine_ahead, back_ref, ahead_ref, out_ref, work_ref
+    table, u_ref, mod_ref, phase_ref, halo_ref, sums_ref, mine_back, mine_ahead, ahead_ref, odd_ref, top_ref, end_ref, out_ref, work_ref
 ):
     half, cols = u_ref.shape[2] // 2, u_ref.shape[3]
     quarter = half // 2
+    back_ref = jnp.concatenate([top_ref[...], end_ref[...]], axis=0) + odd_ref[...]
     summer, rows = Summer(table), Rows(work_ref)
     even_zero, odd_zero, top_zero = local_plane(rows, u_ref, halo_ref, 0)
     zero = plane_views(even_zero, odd_zero, top_zero)
@@ -359,37 +375,48 @@
     )(displacement, element_modulus, element_phase)
     halo = shifted(rim, "gy", 1)
     back_rows, ahead_rows = 10 * half + 8, 5 * half + half // 2
-    back, ahead = pl.pallas_call(
-        pack_kernel,
+    params = pltpu.CompilerParams(vmem_limit_bytes=24 << 20)
+    scratch = [pltpu.VMEM((slots, cols // 128, rows, 128), kind)]
+    ahead_shape = jax.ShapeDtypeStruct((ahead_rows, cols), kind)
+    back_shape = jax.ShapeDtypeStruct((back_rows, cols), kind)
+    part_shape = jax.ShapeDtypeStruct((back_rows // 2, cols), kind)
+    back = pl.pallas_call(
+        back_kernel,
         in_specs=[scalars()] + [whole()] * 5,
-        out_specs=[whole()] * 2,
-        out_shape=[
-            jax.ShapeDtypeStruct((back_rows, cols), kind),
-            jax.ShapeDtypeStruct((ahead_rows, cols), kind),
-        ],
-        scratch_shapes=[pltpu.VMEM((slots, cols // 128, rows, 128), kind)],
-        compiler_params=pltpu.CompilerParams(vmem_limit_bytes=24 << 20),
+        out_specs=whole(),
+        out_shape=back_shape,
+        scratch_shapes=scratch,
+        compiler_params=params,
     )(table, displacement, load, element_modulus, element_phase, halo)
-    from_next = shifted(back, "gx", -1)
+    from_odd = shifted_from(back, "gx", -1, 1)
+    ahead, top, end = pl.pallas_call(
+        ahead_kernel,
+        in_specs=[scalars()] + [whole()] * 5,
+        out_specs=[whole()] * 3,
+        out_shape=[ahead_shape, part_shape, part_shape],
+        scratch_shapes=scratch,
+        compiler_params=params,
+    )(table, displacement, element_modulus, element_phase, halo, back)
     from_last = shifted(ahead, "gx", 1)
+    from_even = [shifted_from(part, "gx", -1, 0) for part in (top, end)]
     sums = pl.pallas_call(
         inner_kernel,
         in_specs=[scalars()] + [whole()] * 5,
         out_specs=whole(),
         out_shape=jax.ShapeDtypeStruct((30, half, cols), kind),
-        scratch_shapes=[pltpu.VMEM((slots, cols // 128, rows, 128), kind)],
-        compiler_params=pltpu.CompilerParams(vmem_limit_bytes=24 << 20),
+        scratch_shapes=scratch,
+        compiler_params=params,
         cost_estimate=pl.CostEstimate(flops=20_000_000, bytes_accessed=1_000_000, transcendentals=0),
     )(table, displacement, load, element_modulus, element_phase, halo)
     return pl.pallas_call(
         finish_kernel,
-        in_specs=[scalars()] + [whole()] * 9,
+        in_specs=[scalars()] + [whole()] * 11,
         out_specs=whole(),
         out_shape=jax.ShapeDtypeStruct(displacement.shape, kind),
-        scratch_shapes=[pltpu.VMEM((slots, cols // 128, rows, 128), kind)],
-        compiler_params=pltpu.CompilerParams(vmem_limit_bytes=24 << 20),
+        scratch_shapes=scratch,
+        compiler_params=params,
     )(
-        table, displacement, element_modulus, element_phase, halo, sums, back, ahead, from_next, from_last
+        table, displacement, element_modulus, element_phase, halo, sums, back, ahead, from_last, from_odd, *from_even
     )
 
 

time: 41.8 us -> 35.4 us (0.85)
  the two profiles are of different devices: /device:TPU:1 before, /device:TPU:62 now
where the time goes in v2:
time: 35.4 us; the launch traced here: 35.2 us
  starting transfers between devices  16.2 us (46%)
  waiting for transfers between devices  10.2 us (29%)
  Pallas kernels  7.91 us (22%)
  local copies, waits for them, and re-layouts  0.77 us (2%)
    ppermute x2, starting transfers between devices, shifted(): lax.ppermute(x, axis, [(i, (i + by) % devices) for i in range(devices)])  10.9 us
    ppermute x2, waiting for transfers between devices, shifted(): lax.ppermute(x, axis, [(i, (i + by) % devices) for i in range(devices)])  8.82 us
    ppermute x3, starting transfers between devices, shifted_from(): lax.ppermute(x, axis, [(i, (i + by) % devices) for i in range(parity, dev...  5.29 us
    pallas_call x1, Pallas kernels, on_device(): pl.pallas_call(finish_kernel, in_specs=[scalars()] + [whole()] * 11, out_...  2.44 us
    pallas_call x1, Pallas kernels, on_device(): pl.pallas_call(inner_kernel, in_specs=[scalars()] + [whole()] * 5, out_sp...  1.63 us
    pallas_call x1, Pallas kernels, on_device(): pl.pallas_call(rim_kernel, grid=(1,), in_specs=[pl.BlockSpec((3, planes,...  1.46 us
    ppermute x3, waiting for transfers between devices, shifted_from(): lax.ppermute(x, axis, [(i, (i + by) % devices) for i in range(parity, dev...  1.39 us
    pallas_call x1, Pallas kernels, on_device(): pl.pallas_call(back_kernel, in_specs=[scalars()] + [whole()] * 5, out_spe...  1.27 us
  transfers between devices with their start and end apart: 5, of which 3 were waited for; matrix products, arithmetic and copies ran while one was open for 2% of the time, Pallas kernels for 8%

profile of v2, /device:TPU:62, one launch (start us, length us, event | category | flops | bytes accessed | tf_op | source)
XLA Modules:
  0.0 35.2 jit_solution(8771408633299491915)
XLA Ops:
  0.0 0.0 copy-start.4
  0.0 1.5 %shard_map.55 = f32[16,256]{1,0:T(8,128)} custom-call(f32[3,2,32,256]{3,2,1,0:T(8,128)} %u_ref.9, f32[2,32,256]{2,1,0:T(8,128)} %mod_ref.9, s32[2,32,256]{2,1,0:T(8,128)} %phase_ref.9), custom_call_target="tpu_custom_call" | custom-call | tf_op jit(solution)/shard_map/pallas_call | solution.py:365
  1.5 1.9 %collective-permute-start = (f32[16,256]{1,0:T(8,128)}, f32[16,256]{1,0:T(8,128)S(1)}, u32[]{:S(2)}, u32[]{:S(2)}) collective-permute-start(f32[16,256]{1,0:T(8,128)} %shard_map.55), channel_id=1, source_target_pairs={{0,1},{1,2},{2,3},{3,4},{4,5},{5,6},{6,7},{7,0},{8,9},{9,10},{10,1... | collective-permute-start | bytes 49160 | tf_op jit(solution)/shard_map/ppermute | solution.py:13
  3.4 0.0 copy-done.4
  3.4 0.0 copy-start.3
  3.4 0.5 %copy.6 = f32[3,8,8,3,3]{4,3,2,1,0:T(4,128)S(1)} copy(f32[3,8,8,3,3]{2,1,4,3,0:T(8,128)S(1)} %copy-done.4) | data formatting | bytes 13824 | tf_op args[4]
  3.9 0.0 copy-start
  3.9 0.0 copy-start.1
  3.9 0.0 copy-start.2
  3.9 0.3 reshape.3.table
  4.2 6.2 %collective-permute-done.halo_ref = f32[16,256]{1,0:T(8,128)S(1)} collective-permute-done((f32[16,256]{1,0:T(8,128)}, f32[16,256]{1,0:T(8,128)S(1)}, u32[]{:S(2)}, u32[]{:S(2)}) %collective-permute-start) | collective-permute-done | bytes 16416 | tf_op jit(solution)/shard_map/ppermute | solution.py:13
  10.4 0.0 copy-done.3
  10.4 0.0 copy-done
  10.4 0.0 copy-done.1
  10.4 0.0 copy-done.2
  10.4 1.3 %shard_map.57.back_ref.mine_back = f32[168,256]{1,0:T(8,128)S(1)} custom-call(f32[1728]{0:T(1024)S(1)} %reshape.3.table, f32[3,2,32,256]{3,2,1,0:T(8,128)S(1)} %copy-done, f32[3,2,32,256]{3,2,1,0:T(8,128)S(1)} %copy-done.3, f32[2,32,256]{2,1,0:T(8,128)S(1)} %copy-done.1, s32[2,32,256]{2,1,0:T(8,128)S(1)} %copy-done.2, ...), custom_call_target="tpu_custom_call" | custom-call | tf_op jit(solution)/shard_map/pallas_call | solution.py:383
  11.7 1.3 %collective-permute-start.2 = (f32[168,256]{1,0:T(8,128)S(1)}, f32[168,256]{1,0:T(8,128)S(1)}, u32[]{:S(2)}, u32[]{:S(2)}) collective-permute-start(f32[168,256]{1,0:T(8,128)S(1)} %shard_map.57.back_ref.mine_back), channel_id=1, source_target_pairs={{8,0},{24,16},{40,32},{56,48},{72,64},{88,80},{104,96},{120,112},{... | collective-permute-start | bytes 516104 | tf_op jit(solution)/shard_map/ppermute | solution.py:18
  13.0 1.1 %shard_map.58 = (f32[88,256]{1,0:T(8,128)S(1)}, f32[84,256]{1,0:T(8,128)S(1)}, f32[84,256]{1,0:T(8,128)S(1)}) custom-call(f32[1728]{0:T(1024)S(1)} %reshape.3.table, f32[3,2,32,256]{3,2,1,0:T(8,128)S(1)} %copy-done, f32[2,32,256]{2,1,0:T(8,128)S(1)} %copy-done.1, s32[2,32,256]{2,1,0:T(8,128)S(1)} %copy-done.2, f32[16,256]{1,0:T(8,128)S(1)} %collective-permute-done.halo_ref, ...), custom_call_target="tpu_custom_call" | custom-call | tf_op jit(solution)/shard_map/pallas_call | solution.py:392
  14.1 9.0 %collective-permute-start.1 = (f32[88,256]{1,0:T(8,128)S(1)}, f32[88,256]{1,0:T(8,128)S(1)}, u32[]{:S(2)}, u32[]{:S(2)}) collective-permute-start(f32[88,256]{1,0:T(8,128)S(1)} %get-tuple-element.8.mine_ahead), channel_id=1, source_target_pairs={{0,8},{8,16},{16,24},{24,32},{32,40},{40,48},{48,56},{56,64},{64,7... | collective-permute-start | bytes 270344 | tf_op jit(solution)/shard_map/ppermute | solution.py:13
  23.2 2.7 %collective-permute-start.3 = (f32[84,256]{1,0:T(8,128)S(1)}, f32[84,256]{1,0:T(8,128)S(1)}, u32[]{:S(2)}, u32[]{:S(2)}) collective-permute-start(f32[84,256]{1,0:T(8,128)S(1)} %get-tuple-element.9), channel_id=1, source_target_pairs={{0,504},{16,8},{32,24},{48,40},{64,56},{80,72},{96,88},{112,104},{... | collective-permute-start | bytes 258056 | tf_op jit(solution)/shard_map/ppermute | solution.py:18
  25.9 1.3 %collective-permute-start.4 = (f32[84,256]{1,0:T(8,128)S(1)}, f32[84,256]{1,0:T(8,128)S(1)}, u32[]{:S(2)}, u32[]{:S(2)}) collective-permute-start(f32[84,256]{1,0:T(8,128)S(1)} %get-tuple-element.10), channel_id=1, source_target_pairs={{0,504},{16,8},{32,24},{48,40},{64,56},{80,72},{96,88},{112,104},{... | collective-permute-start | bytes 258056 | tf_op jit(solution)/shard_map/ppermute | solution.py:18
  27.2 1.6 %shard_map.56.sums_ref = f32[30,16,256]{2,1,0:T(8,128)S(1)} custom-call(f32[1728]{0:T(1024)S(1)} %reshape.3.table, f32[3,2,32,256]{3,2,1,0:T(8,128)S(1)} %copy-done, f32[3,2,32,256]{3,2,1,0:T(8,128)S(1)} %copy-done.3, f32[2,32,256]{2,1,0:T(8,128)S(1)} %copy-done.1, s32[2,32,256]{2,1,0:T(8,128)S(1)} %copy-done.2, f32[16,256]{1,0:T(8,128)S(1)} %collective-permute-done.halo_ref), custom_call_target="tpu_custom_call" | custom-call | flops 20000000 | bytes 1000000 | tf_op jit(solution)/shard_map/pallas_call | solution.py:402
  28.8 0.0 collective-permute-done.3.top_ref
  28.8 1.4 %collective-permute-done.4.end_ref = f32[84,256]{1,0:T(8,128)S(1)} collective-permute-done((f32[84,256]{1,0:T(8,128)S(1)}, f32[84,256]{1,0:T(8,128)S(1)}, u32[]{:S(2)}, u32[]{:S(2)}) %collective-permute-start.4) | collective-permute-done | bytes 86048 | tf_op jit(solution)/shard_map/ppermute | solution.py:18
  30.2 2.6 %collective-permute-done.1.ahead_ref = f32[88,256]{1,0:T(8,128)S(1)} collective-permute-done((f32[88,256]{1,0:T(8,128)S(1)}, f32[88,256]{1,0:T(8,128)S(1)}, u32[]{:S(2)}, u32[]{:S(2)}) %collective-permute-start.1) | collective-permute-done | bytes 90144 | tf_op jit(solution)/shard_map/ppermute | solution.py:13
  32.8 0.0 collective-permute-done.2.odd_ref
  32.8 2.4 %shard_map.59 = f32[3,2,32,256]{3,2,1,0:T(8,128)} custom-call(f32[1728]{0:T(1024)S(1)} %reshape.3.table, f32[3,2,32,256]{3,2,1,0:T(8,128)S(1)} %copy-done, f32[2,32,256]{2,1,0:T(8,128)S(1)} %copy-done.1, s32[2,32,256]{2,1,0:T(8,128)S(1)} %copy-done.2, f32[16,256]{1,0:T(8,128)S(1)} %collective-permute-done.halo_ref, f32[30,16,256]{2,1,0:T(8,128)S(1)} %shard_map.56.sums_ref, ...), custom_call_target="tpu_custom_call" | custom-call | tf_op jit(solution)/shard_map/pallas_call | solution.py:411
Async XLA Ops:
  0.0 3.4 %copy-start.4 = (f32[3,8,8,3,3]{2,1,4,3,0:T(8,128)S(1)}, f32[3,8,8,3,3]{2,1,4,3,0:T(8,128)}, u32[]{:S(2)}) copy-start(f32[3,8,8,3,3]{2,1,4,3,0:T(8,128)} %param.9) | copy-start | bytes 20740
  1.5 9.0 %collective-permute-start = (f32[16,256]{1,0:T(8,128)}, f32[16,256]{1,0:T(8,128)S(1)}, u32[]{:S(2)}, u32[]{:S(2)}) collective-permute-start(f32[16,256]{1,0:T(8,128)} %shard_map.55), channel_id=1, source_target_pairs={{0,1},{1,2},{2,3},{3,4},{4,5},{5,6},{6,7},{7,0},{8,9},{9,10},{10,1... | collective-permute-start | bytes 49160 | tf_op jit(solution)/shard_map/ppermute | solution.py:13
  3.4 7.0 %copy-start.3 = (f32[3,2,32,256]{3,2,1,0:T(8,128)S(1)}, f32[3,2,32,256]{3,2,1,0:T(8,128)}, u32[]{:S(2)}) copy-start(f32[3,2,32,256]{3,2,1,0:T(8,128)} %load_ref.3) | copy-start | bytes 589828
  3.9 6.5 %copy-start = (f32[3,2,32,256]{3,2,1,0:T(8,128)S(1)}, f32[3,2,32,256]{3,2,1,0:T(8,128)}, u32[]{:S(2)}) copy-start(f32[3,2,32,256]{3,2,1,0:T(8,128)} %u_ref.9) | copy-start | bytes 589828
  3.9 6.5 %copy-start.1 = (f32[2,32,256]{2,1,0:T(8,128)S(1)}, f32[2,32,256]{2,1,0:T(8,128)}, u32[]{:S(2)}) copy-start(f32[2,32,256]{2,1,0:T(8,128)} %mod_ref.9) | copy-start | bytes 196612
  3.9 6.5 %copy-start.2 = (s32[2,32,256]{2,1,0:T(8,128)S(1)}, s32[2,32,256]{2,1,0:T(8,128)}, u32[]{:S(2)}) copy-start(s32[2,32,256]{2,1,0:T(8,128)} %phase_ref.9) | copy-start | bytes 196612
  11.7 21.1 %collective-permute-start.2 = (f32[168,256]{1,0:T(8,128)S(1)}, f32[168,256]{1,0:T(8,128)S(1)}, u32[]{:S(2)}, u32[]{:S(2)}) collective-permute-start(f32[168,256]{1,0:T(8,128)S(1)} %shard_map.57.back_ref.mine_back), channel_id=1, source_target_pairs={{8,0},{24,16},{40,32},{56,48},{72,64},{88,80},{104,96},{120,112},{... | collective-permute-start | bytes 516104 | tf_op jit(solution)/shard_map/ppermute | solution.py:18
  14.1 18.6 %collective-permute-start.1 = (f32[88,256]{1,0:T(8,128)S(1)}, f32[88,256]{1,0:T(8,128)S(1)}, u32[]{:S(2)}, u32[]{:S(2)}) collective-permute-start(f32[88,256]{1,0:T(8,128)S(1)} %get-tuple-element.8.mine_ahead), channel_id=1, source_target_pairs={{0,8},{8,16},{16,24},{24,32},{32,40},{40,48},{48,56},{56,64},{64,7... | collective-permute-start | bytes 270344 | tf_op jit(solution)/shard_map/ppermute | solution.py:13
  23.2 5.6 %collective-permute-start.3 = (f32[84,256]{1,0:T(8,128)S(1)}, f32[84,256]{1,0:T(8,128)S(1)}, u32[]{:S(2)}, u32[]{:S(2)}) collective-permute-start(f32[84,256]{1,0:T(8,128)S(1)} %get-tuple-element.9), channel_id=1, source_target_pairs={{0,504},{16,8},{32,24},{48,40},{64,56},{80,72},{96,88},{112,104},{... | collective-permute-start | bytes 258056 | tf_op jit(solution)/shard_map/ppermute | solution.py:18
  25.9 4.3 %collective-permute-start.4 = (f32[84,256]{1,0:T(8,128)S(1)}, f32[84,256]{1,0:T(8,128)S(1)}, u32[]{:S(2)}, u32[]{:S(2)}) collective-permute-start(f32[84,256]{1,0:T(8,128)S(1)} %get-tuple-element.10), channel_id=1, source_target_pairs={{0,504},{16,8},{32,24},{48,40},{64,56},{80,72},{96,88},{112,104},{... | collective-permute-start | bytes 258056 | tf_op jit(solution)/shard_map/ppermute | solution.py:18

commit v3 on v2

--- a/solution.py
+++ b/solution.py
@@ -70,29 +70,41 @@
 
 class Elements:
     def __init__(self, modulus, phase):
-        self.modulus = tiles(modulus)
-        self.phase = tiles(phase)
+        phase = tiles(phase)
+        self.modulus, self.first, self.second = tiles(modulus), phase == 0, phase == 1
+
+
+def coefficient(corner, partner, kind, i, j):
+    return ((corner * 4 + partner) * 2 + ("0s1o".index(kind) // 2)) * 9 + i * 3 + j
+
+
+PHASE_ROWS = 4 * 4 * 2 * 9
+
+
+def fill_coefficients(table, tiles_ref):
+    even = even_lanes((8, 128))
+    for ph in range(3):
+        for corner in range(4):
+            for partner in range(4):
+                for kind in "so" if partner % 2 == corner % 2 else "01":
+                    for i in range(3):
+                        for j in range(3):
+                            places = [
+                                table[(((ph * 8 + corner * 2 + parity) * 8 + partner * 2 + side) * 3 + i) * 3 + j]
+                                for parity, side in enumerate(PARITY[kind])
+                            ]
+                            row = ph * PHASE_ROWS + coefficient(corner, partner, kind, i, j)
+                            tiles_ref[row] = jnp.where(even, places[0], places[1])
 
 
 class Summer:
-    def __init__(self, table):
-        self.table = table
-        self.even = even_lanes((8, 128))
-        self.corners = 8
+    def __init__(self, tiles_ref):
+        self.tiles = tiles_ref
 
     def entry(self, elements, corner, partner, kind, i, j):
-        first, second = PARITY[kind]
-        picked = []
-        for ph in range(3):
-            places = []
-            for parity, side in ((0, first), (1, second)):
-                c = corner * 2 + parity
-                d = partner * 2 + side
-                places.append(self.table[(((ph * 8 + c) * 8 + d) * 3 + i) * 3 + j])
-            picked.append(jnp.where(self.even, places[0], places[1])[None])
-        return jnp.where(
-            elements.phase == 0, picked[0], jnp.where(elements.phase == 1, picked[1], picked[2])
-        )
+        row = coefficient(corner, partner, kind, i, j)
+        picked = [self.tiles[ph * PHASE_ROWS + row][None] for ph in range(3)]
+        return jnp.where(elements.first, picked[0], jnp.where(elements.second, picked[1], picked[2]))
 
     def force(self, elements, corner, terms):
         total = [None] * 3
@@ -178,10 +190,14 @@
         return jnp.concatenate([self.work[slot, k] for k in range(parts)], axis=1)
 
 
+def halo_row(halo_ref, row, cols):
+    return jnp.zeros((1, cols), jnp.float32) if halo_ref is None else halo_ref[row : row + 1, :]
+
+
 def local_plane(rows, u_ref, halo_ref, plane):
     split = [rows.split(u_ref[c, plane]) for c in range(3)]
     even, odd = [a for a, _ in split], [b for _, b in split]
-    tops = [halo_ref[3 * plane + c : 3 * plane + c + 1, :] for c in range(3)]
+    tops = [halo_row(halo_ref, 3 * plane + c, u_ref.shape[-1]) for c in range(3)]
     return even, odd, tops
 
 
@@ -189,74 +205,117 @@
     split = [rows.split(mod_ref[plane]), rows.split(phase_ref[plane].astype(jnp.float32))]
     even, odd = [a for a, _ in split], [b for _, b in split]
     before = (
-        down_row(odd[0], halo_ref[6 + plane : 7 + plane, :]),
-        down_row(odd[1], halo_ref[8 + plane : 9 + plane, :]),
+        down_row(odd[0], halo_row(halo_ref, 6 + plane, mod_ref.shape[-1])),
+        down_row(odd[1], halo_row(halo_ref, 8 + plane, mod_ref.shape[-1])),
     )
     return even, before
 
 
-def rim_kernel(u_ref, mod_ref, phase_ref, out_ref):
-    out_ref[...] = jnp.zeros(out_ref.shape, jnp.float32)
+def fetch_kernel(u_hbm, load_hbm, mod_hbm, phase_hbm, out_ref, u_ref, load_ref, mod_ref, phase_ref, sems):
+    copies = [
+        pltpu.make_async_copy(source, target, sems.at[k])
+        for k, (source, target) in enumerate(
+            ((u_hbm, u_ref), (mod_hbm, mod_ref), (phase_hbm, phase_ref), (load_hbm, load_ref))
+        )
+    ]
+    for copy in copies:
+        copy.start()
+    for copy in copies[:3]:
+        copy.wait()
+    last = u_ref.shape[2] - 1
     for plane in range(2):
         for c in range(3):
-            out_ref[3 * plane + c : 3 * plane + c + 1, :] = u_ref[c, plane, 7:8, :]
-        out_ref[6 + plane : 7 + plane, :] = mod_ref[plane, 7:8, :]
-        out_ref[8 + plane : 9 + plane, :] = phase_ref[plane, 7:8, :].astype(jnp.float32)
-
-
-def ahead_kernel(table, u_ref, mod_ref, phase_ref, halo_ref, back_ref, ahead_ref, top_ref, end_ref, work_ref):
+            out_ref[3 * plane + c : 3 * plane + c + 1, :] = u_ref[c, plane, last : last + 1, :]
+        out_ref[6 + plane : 7 + plane, :] = mod_ref[plane, last : last + 1, :]
+        out_ref[8 + plane : 9 + plane, :] = phase_ref[plane, last : last + 1, :].astype(jnp.float32)
+    out_ref[10:16, :] = jnp.zeros((6, out_ref.shape[1]), jnp.float32)
+    copies[3].wait()
+
+
+def prepare_kernel(table, u_ref, load_ref, mod_ref, phase_ref, tiles_ref, back_ref, ahead_ref, work_ref):
     half, cols = u_ref.shape[2] // 2, u_ref.shape[3]
     quarter = half // 2
-    summer, rows = Summer(table), Rows(work_ref)
-    top_ref[...] = back_ref[: top_ref.shape[0], :]
-    end_ref[...] = back_ref[top_ref.shape[0] :, :]
-    one = plane_views(*local_plane(rows, u_ref, halo_ref, 1))
-    rows_one = element_rows(rows, mod_ref, phase_ref, halo_ref, 1)
+    fill_coefficients(table, tiles_ref)
+    summer, rows = Summer(tiles_ref), Rows(work_ref)
+    even_zero, odd_zero, top_zero = local_plane(rows, u_ref, None, 0)
+    zero = plane_views(even_zero, odd_zero, top_zero)
+    one = plane_views(*local_plane(rows, u_ref, None, 1))
+    rows_zero = element_rows(rows, mod_ref, phase_ref, None, 0)
+    rows_one = element_rows(rows, mod_ref, phase_ref, None, 1)
     even = even_lanes((half, cols))
-    beyond = None
-    for cy in range(2):
-        elements = Elements(*rows_one[cy])
-        part = summer.force(elements, 2 + cy, terms_of(one, 1, cy, 0, "so"))
-        beyond = part if beyond is None else added(beyond, part)
-        for k in range(2):
-            start = half + quarter + (2 * k + cy) * half
-            ahead_ref[start : start + half, :] = rows_one[cy][k]
-    beyond = at_nodes(beyond, cols)
-    ahead_ref[0:half, :] = jnp.where(even, beyond[0], last_lane(beyond[1]))
-    ahead_ref[half : half + quarter, :] = jnp.where(
-        even[:quarter], beyond[2][:quarter], last_lane(beyond[2][quarter:])
-    )
-
-
-def back_kernel(table, u_ref, load_ref, mod_ref, phase_ref, halo_ref, back_ref, work_ref):
-    half, cols = u_ref.shape[2] // 2, u_ref.shape[3]
-    summer, rows = Summer(table), Rows(work_ref)
-    even_zero, odd_zero, top_zero = local_plane(rows, u_ref, halo_ref, 0)
-    zero = plane_views(even_zero, odd_zero, top_zero)
-    one = plane_views(*local_plane(rows, u_ref, halo_ref, 1))
-    rows_zero = element_rows(rows, mod_ref, phase_ref, halo_ref, 0)
-    even = even_lanes((half, cols))
-    own = None
+    own, beyond = None, None
     for cy in range(2):
         elements = Elements(*rows_zero[cy])
         part = summer.force(
             elements, cy, terms_of(zero, 0, cy, 0, "o") + terms_of(one, 0, cy, 1, "so")
         )
         own = part if own is None else added(own, part)
+        elements = Elements(*rows_one[cy])
+        part = summer.force(elements, 2 + cy, terms_of(one, 1, cy, 0, "so"))
+        beyond = part if beyond is None else added(beyond, part)
         for k in range(2):
-            back_ref[(6 + 2 * k + cy) * half : (7 + 2 * k + cy) * half, :] = rows_zero[cy][k]
-    own = at_nodes(own, cols)
+            start = (6 + 2 * k + cy) * half
+            back_ref[start : start + half, :] = rows_zero[cy][k]
+            start = half + quarter + (2 * k + cy) * half
+            ahead_ref[start : start + half, :] = rows_one[cy][k]
+    own, beyond = at_nodes(own, cols), at_nodes(beyond, cols)
     back_ref[10 * half :, :] = jnp.zeros((8, cols), jnp.float32)
     for c in range(3):
         left = rows.split(load_ref[c, 0])[0] - own[c]
         back_ref[c * half : (c + 1) * half, :] = jnp.where(even, left, even_zero[c])
         back_ref[(3 + c) * half : (4 + c) * half, :] = odd_zero[c]
-        back_ref[10 * half + c : 10 * half + c + 1, :] = top_zero[c]
-
-
-def inner_kernel(table, u_ref, load_ref, mod_ref, phase_ref, halo_ref, sums_ref, work_ref):
+    ahead_ref[0:half, :] = jnp.where(even, beyond[0], last_lane(beyond[1]))
+    ahead_ref[half : half + quarter, :] = jnp.where(
+        even[:quarter], beyond[2][:quarter], last_lane(beyond[2][quarter:])
+    )
+
+
+def top_kernel(
+    tiles_ref, u_ref, halo_ref, back_in, ahead_in, back_ref, ahead_ref, first_ref, second_ref
+):
     half, cols = u_ref.shape[2] // 2, u_ref.shape[3]
-    summer, rows = Summer(table), Rows(work_ref)
+    quarter = half // 2
+    summer = Summer(tiles_ref)
+
+    def wide(row):
+        return jnp.broadcast_to(row, (8, cols))
+
+    views, corners = [], []
+    for plane in range(2):
+        before = [wide(halo_ref[3 * plane + c : 3 * plane + c + 1, :]) for c in range(3)]
+        same = [wide(u_ref[c, plane, 0:1, :]) for c in range(3)]
+        views.append(([pair_even(a) for a in same], None, [pair_odd(a) for a in before]))
+        corners.append(
+            Elements(wide(halo_ref[6 + plane : 7 + plane, :]), wide(halo_ref[8 + plane : 9 + plane, :]))
+        )
+    own = summer.force(
+        corners[0], 1, terms_of(views[0], 0, 1, 0, "o") + terms_of(views[1], 0, 1, 1, "so")
+    )
+    beyond = summer.force(corners[1], 3, terms_of(views[1], 1, 1, 0, "so"))
+    own, beyond = at_nodes(own, cols), at_nodes(beyond, cols)
+    even = even_lanes((1, cols))
+    back_ref[...] = back_in[...]
+    ahead_ref[...] = ahead_in[...]
+    for c in range(3):
+        old = back_in[c * half : c * half + 1, :]
+        back_ref[c * half : c * half + 1, :] = jnp.where(even, old - own[c][0:1], old)
+    back_ref[10 * half : 10 * half + 3, :] = halo_ref[0:3, :]
+    for k in range(2):
+        start = (7 + 2 * k) * half
+        back_ref[start : start + 1, :] = halo_ref[6 + 2 * k : 7 + 2 * k, :]
+        start = half + quarter + (2 * k + 1) * half
+        ahead_ref[start : start + 1, :] = halo_ref[7 + 2 * k : 8 + 2 * k, :]
+    ahead_ref[0:1, :] = ahead_in[0:1, :] + jnp.where(even, beyond[0][0:1], last_lane(beyond[1])[0:1])
+    ahead_ref[half : half + 1, :] = jnp.where(
+        even, ahead_in[half : half + 1, :] + beyond[2][0:1], ahead_in[half : half + 1, :]
+    )
+    first_ref[...] = back_ref[: first_ref.shape[0], :]
+    second_ref[...] = back_ref[first_ref.shape[0] :, :]
+
+
+def inner_kernel(tiles_ref, u_ref, load_ref, mod_ref, phase_ref, halo_ref, sums_ref, work_ref):
+    half, cols = u_ref.shape[2] // 2, u_ref.shape[3]
+    summer, rows = Summer(tiles_ref), Rows(work_ref)
     zero = plane_views(*local_plane(rows, u_ref, halo_ref, 0))
     one = plane_views(*local_plane(rows, u_ref, halo_ref, 1))
     rows_zero = element_rows(rows, mod_ref, phase_ref, halo_ref, 0)
@@ -293,12 +352,12 @@
 
 
 def finish_kernel(
-    table, u_ref, mod_ref, phase_ref, halo_ref, sums_ref, mine_back, mine_ahead, ahead_ref, odd_ref, top_ref, end_ref, out_ref, work_ref
+    tiles_ref, u_ref, mod_ref, phase_ref, halo_ref, sums_ref, mine_back, mine_ahead, ahead_ref, odd_ref, top_ref, end_ref, out_ref, work_ref
 ):
     half, cols = u_ref.shape[2] // 2, u_ref.shape[3]
     quarter = half // 2
     back_ref = jnp.concatenate([top_ref[...], end_ref[...]], axis=0) + odd_ref[...]
-    summer, rows = Summer(table), Rows(work_ref)
+    summer, rows = Summer(tiles_ref), Rows(work_ref)
     even_zero, odd_zero, top_zero = local_plane(rows, u_ref, halo_ref, 0)
     zero = plane_views(even_zero, odd_zero, top_zero)
     rows_zero = element_rows(rows, mod_ref, phase_ref, halo_ref, 0)
@@ -360,19 +419,17 @@
     half = rows // 2
     kind = displacement.dtype
     table = stiffness.reshape(-1)
-    last = rows // 8 - 1
     slots = 16
-    rim = pl.pallas_call(
-        rim_kernel,
-        grid=(1,),
-        in_specs=[
-            pl.BlockSpec((3, planes, 8, cols), lambda i: (0, 0, last, 0)),
-            pl.BlockSpec((planes, 8, cols), lambda i: (0, last, 0)),
-            pl.BlockSpec((planes, 8, cols), lambda i: (0, last, 0)),
-        ],
-        out_specs=pl.BlockSpec((16, cols), lambda i: (0, 0)),
-        out_shape=jax.ShapeDtypeStruct((16, cols), kind),
-    )(displacement, element_modulus, element_phase)
+    rim, displacement, load, element_modulus, element_phase = pl.pallas_call(
+        fetch_kernel,
+        in_specs=[pl.BlockSpec(memory_space=pl.ANY)] * 4,
+        out_specs=[whole()] * 5,
+        out_shape=[jax.ShapeDtypeStruct((16, cols), kind)]
+        + [jax.ShapeDtypeStruct(a.shape, a.dtype) for a in (displacement, load, element_modulus, element_phase)],
+        scratch_shapes=[pltpu.SemaphoreType.DMA((4,))],
+        compiler_params=pltpu.CompilerParams(vmem_limit_bytes=8 << 20),
+        cost_estimate=pl.CostEstimate(flops=1_000_000_000, bytes_accessed=0, transcendentals=0),
+    )(*(pltpu.with_memory_space_constraint(a, pltpu.HBM) for a in (displacement, load, element_modulus, element_phase)))
     halo = shifted(rim, "gy", 1)
     back_rows, ahead_rows = 10 * half + 8, 5 * half + half // 2
     params = pltpu.CompilerParams(vmem_limit_bytes=24 << 20)
@@ -380,43 +437,44 @@
     ahead_shape = jax.ShapeDtypeStruct((ahead_rows, cols), kind)
     back_shape = jax.ShapeDtypeStruct((back_rows, cols), kind)
     part_shape = jax.ShapeDtypeStruct((back_rows // 2, cols), kind)
-    back = pl.pallas_call(
-        back_kernel,
-        in_specs=[scalars()] + [whole()] * 5,
-        out_specs=whole(),
-        out_shape=back_shape,
+    tile_shape = jax.ShapeDtypeStruct((3 * PHASE_ROWS, 8, 128), kind)
+    coefficients, back, ahead = pl.pallas_call(
+        prepare_kernel,
+        in_specs=[scalars()] + [whole()] * 4,
+        out_specs=[whole()] * 3,
+        out_shape=[tile_shape, back_shape, ahead_shape],
         scratch_shapes=scratch,
         compiler_params=params,
-    )(table, displacement, load, element_modulus, element_phase, halo)
+        cost_estimate=pl.CostEstimate(flops=20_000_000, bytes_accessed=6_000_000, transcendentals=0),
+    )(table, displacement, load, element_modulus, element_phase)
+    back, ahead, top, end = pl.pallas_call(
+        top_kernel,
+        in_specs=[whole()] * 5,
+        out_specs=[whole()] * 4,
+        out_shape=[back_shape, ahead_shape, part_shape, part_shape],
+        compiler_params=params,
+    )(coefficients, displacement, halo, back, ahead)
     from_odd = shifted_from(back, "gx", -1, 1)
-    ahead, top, end = pl.pallas_call(
-        ahead_kernel,
-        in_specs=[scalars()] + [whole()] * 5,
-        out_specs=[whole()] * 3,
-        out_shape=[ahead_shape, part_shape, part_shape],
-        scratch_shapes=scratch,
-        compiler_params=params,
-    )(table, displacement, element_modulus, element_phase, halo, back)
     from_last = shifted(ahead, "gx", 1)
     from_even = [shifted_from(part, "gx", -1, 0) for part in (top, end)]
     sums = pl.pallas_call(
         inner_kernel,
-        in_specs=[scalars()] + [whole()] * 5,
+        in_specs=[whole()] * 6,
         out_specs=whole(),
         out_shape=jax.ShapeDtypeStruct((30, half, cols), kind),
         scratch_shapes=scratch,
         compiler_params=params,
         cost_estimate=pl.CostEstimate(flops=20_000_000, bytes_accessed=1_000_000, transcendentals=0),
-    )(table, displacement, load, element_modulus, element_phase, halo)
+    )(coefficients, displacement, load, element_modulus, element_phase, halo)
     return pl.pallas_call(
         finish_kernel,
-        in_specs=[scalars()] + [whole()] * 11,
+        in_specs=[whole()] * 12,
         out_specs=whole(),
         out_shape=jax.ShapeDtypeStruct(displacement.shape, kind),
         scratch_shapes=scratch,
         compiler_params=params,
     )(
-        table, displacement, element_modulus, element_phase, halo, sums, back, ahead, from_last, from_odd, *from_even
+        coefficients, displacement, element_modulus, element_phase, halo, sums, back, ahead, from_last, from_odd, *from_even
     )
 
 

time: 35.4 us -> 33.6 us (0.949)
  the two profiles are of different devices: /device:TPU:62 before, /device:TPU:1 now
where the time goes in v3:
time: 33.6 us; the launch traced here: 33.4 us
  starting transfers between devices  23.2 us (69%)
  Pallas kernels  5.51 us (16%)
  waiting for transfers between devices  3.9 us (12%)
  local copies, waits for them, and re-layouts  0.76 us (2%)
    ppermute x2, starting transfers between devices, shifted(): lax.ppermute(x, axis, [(i, (i + by) % devices) for i in range(devices)])  13.6 us
    ppermute x3, starting transfers between devices, shifted_from(): lax.ppermute(x, axis, [(i, (i + by) % devices) for i in range(parity, dev...  9.6 us
    ppermute x2, waiting for transfers between devices, shifted(): lax.ppermute(x, axis, [(i, (i + by) % devices) for i in range(devices)])  3.16 us
    pallas_call x1, Pallas kernels, on_device(): pl.pallas_call(prepare_kernel, in_specs=[scalars()] + [whole()] * 4, out_...  1.72 us
    pallas_call x1, Pallas kernels, on_device(): pl.pallas_call(finish_kernel, in_specs=[whole()] * 12, out_specs=whole(),...  1.59 us
    pallas_call x1, Pallas kernels, on_device(): pl.pallas_call(fetch_kernel, in_specs=[pl.BlockSpec(memory_space=pl.ANY)]...  1.15 us
    pallas_call x1, Pallas kernels, on_device(): pl.pallas_call(inner_kernel, in_specs=[whole()] * 6, out_specs=whole(), o...  0.8 us
    ppermute x3, waiting for transfers between devices, shifted_from(): lax.ppermute(x, axis, [(i, (i + by) % devices) for i in range(parity, dev...  0.74 us
  transfers between devices with their start and end apart: 5, of which 3 were waited for; matrix products, arithmetic and copies ran while one was open for 2% of the time, Pallas kernels for 8%

profile of v3, /device:TPU:1, one launch (start us, length us, event | category | flops | bytes accessed | tf_op | source)
XLA Modules:
  0.0 33.4 jit_solution(8591728684824895875)
XLA Ops:
  0.0 0.0 copy-start
  0.0 1.2 %shard_map.55 = (f32[16,256]{1,0:T(8,128)S(1)}, f32[3,2,32,256]{3,2,1,0:T(8,128)S(1)}, f32[3,2,32,256]{3,2,1,0:T(8,128)S(1)}, f32[2,32,256]{2,1,0:T(8,128)S(1)}, s32[2,32,256]{2,1,0:T(8,128)S(1)}) custom-call(f32[3,2,32,256]{3,2,1,0:T(8,128)} %u_hbm.1, f32[3,2,32,256]{3,2,1,0:T(8,128)} %load_hbm.1, f32[2,32,256]{2,1,0:T(8,128)} %mod_hbm.1, ...), custom_call_target="tpu_custom_call" | custom-call | flops 1000000000 | tf_op jit(solution)/shard_map/pallas_call | solution.py:423
  1.2 5.4 %collective-permute-start = (f32[16,256]{1,0:T(8,128)S(1)}, f32[16,256]{1,0:T(8,128)S(1)}, u32[]{:S(2)}, u32[]{:S(2)}) collective-permute-start(f32[16,256]{1,0:T(8,128)S(1)} %get-tuple-element.22), channel_id=1, source_target_pairs={{0,1},{1,2},{2,3},{3,4},{4,5},{5,6},{6,7},{7,0},{8,9},{9,10},{10,1... | collective-permute-start | bytes 49160 | tf_op jit(solution)/shard_map/ppermute | solution.py:13
  6.6 0.0 copy-done
  6.6 0.5 %copy.6 = f32[3,8,8,3,3]{4,3,2,1,0:T(4,128)S(1)} copy(f32[3,8,8,3,3]{2,1,4,3,0:T(8,128)S(1)} %copy-done) | data formatting | bytes 13824 | tf_op args[4]
  7.1 0.3 reshape.3.table
  7.3 1.7 %shard_map.56 = (f32[864,8,128]{2,1,0:T(8,128)S(1)}, f32[168,256]{1,0:T(8,128)S(1)}, f32[88,256]{1,0:T(8,128)S(1)}) custom-call(f32[1728]{0:T(1024)S(1)} %reshape.3.table, f32[3,2,32,256]{3,2,1,0:T(8,128)S(1)} %get-tuple-element.17.u_ref, f32[3,2,32,256]{3,2,1,0:T(8,128)S(1)} %get-tuple-element.18.load_ref, f32[2,32,256]{2,1,0:T(8,128)S(1)} %get-tuple-element.19.mod_ref, ...), custom_call_target="tpu_custom_call" | custom-call | flops 20000000 | bytes 6000000 | tf_op jit(solution)/shard_map/pallas_call | solution.py:441
  9.1 1.6 %collective-permute-done.halo_ref = f32[16,256]{1,0:T(8,128)S(1)} collective-permute-done((f32[16,256]{1,0:T(8,128)S(1)}, f32[16,256]{1,0:T(8,128)S(1)}, u32[]{:S(2)}, u32[]{:S(2)}) %collective-permute-start) | collective-permute-done | bytes 16416 | tf_op jit(solution)/shard_map/ppermute | solution.py:13
  10.6 0.3 shard_map.58
  10.9 1.3 %collective-permute-start.2 = (f32[168,256]{1,0:T(8,128)S(1)}, f32[168,256]{1,0:T(8,128)S(1)}, u32[]{:S(2)}, u32[]{:S(2)}) collective-permute-start(f32[168,256]{1,0:T(8,128)S(1)} %get-tuple-element.25.mine_back), channel_id=1, source_target_pairs={{8,0},{24,16},{40,32},{56,48},{72,64},{88,80},{104,96},{120,112},{... | collective-permute-start | bytes 516104 | tf_op jit(solution)/shard_map/ppermute | solution.py:18
  12.2 8.2 %collective-permute-start.1 = (f32[88,256]{1,0:T(8,128)S(1)}, f32[88,256]{1,0:T(8,128)S(1)}, u32[]{:S(2)}, u32[]{:S(2)}) collective-permute-start(f32[88,256]{1,0:T(8,128)S(1)} %get-tuple-element.26.mine_ahead), channel_id=1, source_target_pairs={{0,8},{8,16},{16,24},{24,32},{32,40},{40,48},{48,56},{56,64},{64,7... | collective-permute-start | bytes 270344 | tf_op jit(solution)/shard_map/ppermute | solution.py:13
  20.4 7.0 %collective-permute-start.3 = (f32[84,256]{1,0:T(8,128)S(1)}, f32[84,256]{1,0:T(8,128)S(1)}, u32[]{:S(2)}, u32[]{:S(2)}) collective-permute-start(f32[84,256]{1,0:T(8,128)S(1)} %get-tuple-element.27), channel_id=1, source_target_pairs={{0,504},{16,8},{32,24},{48,40},{64,56},{80,72},{96,88},{112,104},{... | collective-permute-start | bytes 258056 | tf_op jit(solution)/shard_map/ppermute | solution.py:18
  27.4 1.3 %collective-permute-start.4 = (f32[84,256]{1,0:T(8,128)S(1)}, f32[84,256]{1,0:T(8,128)S(1)}, u32[]{:S(2)}, u32[]{:S(2)}) collective-permute-start(f32[84,256]{1,0:T(8,128)S(1)} %get-tuple-element.28), channel_id=1, source_target_pairs={{0,504},{16,8},{32,24},{48,40},{64,56},{80,72},{96,88},{112,104},{... | collective-permute-start | bytes 258056 | tf_op jit(solution)/shard_map/ppermute | solution.py:18
  28.7 0.8 %shard_map.57.sums_ref = f32[30,16,256]{2,1,0:T(8,128)S(1)} custom-call(f32[864,8,128]{2,1,0:T(8,128)S(1)} %get-tuple-element.21.tiles_ref, f32[3,2,32,256]{3,2,1,0:T(8,128)S(1)} %get-tuple-element.17.u_ref, f32[3,2,32,256]{3,2,1,0:T(8,128)S(1)} %get-tuple-element.18.load_ref, f32[2,32,256]{2,1,0:T(8,128)S(1)} %get-tuple-element.19.mod_ref, ...), custom_call_target="tpu_custom_call" | custom-call | flops 20000000 | bytes 1000000 | tf_op jit(solution)/shard_map/pallas_call | solution.py:460
  29.5 0.0 collective-permute-done.3.top_ref
  29.5 0.7 %collective-permute-done.4.end_ref = f32[84,256]{1,0:T(8,128)S(1)} collective-permute-done((f32[84,256]{1,0:T(8,128)S(1)}, f32[84,256]{1,0:T(8,128)S(1)}, u32[]{:S(2)}, u32[]{:S(2)}) %collective-permute-start.4) | collective-permute-done | bytes 86048 | tf_op jit(solution)/shard_map/ppermute | solution.py:18
  30.2 1.6 %collective-permute-done.1.ahead_ref = f32[88,256]{1,0:T(8,128)S(1)} collective-permute-done((f32[88,256]{1,0:T(8,128)S(1)}, f32[88,256]{1,0:T(8,128)S(1)}, u32[]{:S(2)}, u32[]{:S(2)}) %collective-permute-start.1) | collective-permute-done | bytes 90144 | tf_op jit(solution)/shard_map/ppermute | solution.py:13
  31.8 0.0 collective-permute-done.2.odd_ref
  31.8 1.6 %shard_map.59 = f32[3,2,32,256]{3,2,1,0:T(8,128)} custom-call(f32[864,8,128]{2,1,0:T(8,128)S(1)} %get-tuple-element.21.tiles_ref, f32[3,2,32,256]{3,2,1,0:T(8,128)S(1)} %get-tuple-element.17.u_ref, f32[2,32,256]{2,1,0:T(8,128)S(1)} %get-tuple-element.19.mod_ref, s32[2,32,256]{2,1,0:T(8,128)S(1)} %get-tuple-element.20.phase_ref, ...), custom_call_target="tpu_custom_call" | custom-call | tf_op jit(solution)/shard_map/pallas_call | solution.py:469
Async XLA Ops:
  0.0 6.6 %copy-start = (f32[3,8,8,3,3]{2,1,4,3,0:T(8,128)S(1)}, f32[3,8,8,3,3]{2,1,4,3,0:T(8,128)}, u32[]{:S(2)}) copy-start(f32[3,8,8,3,3]{2,1,4,3,0:T(8,128)} %param.9) | copy-start | bytes 20740
  1.2 9.5 %collective-permute-start = (f32[16,256]{1,0:T(8,128)S(1)}, f32[16,256]{1,0:T(8,128)S(1)}, u32[]{:S(2)}, u32[]{:S(2)}) collective-permute-start(f32[16,256]{1,0:T(8,128)S(1)} %get-tuple-element.22), channel_id=1, source_target_pairs={{0,1},{1,2},{2,3},{3,4},{4,5},{5,6},{6,7},{7,0},{8,9},{9,10},{10,1... | collective-permute-start | bytes 49160 | tf_op jit(solution)/shard_map/ppermute | solution.py:13
  10.9 21.0 %collective-permute-start.2 = (f32[168,256]{1,0:T(8,128)S(1)}, f32[168,256]{1,0:T(8,128)S(1)}, u32[]{:S(2)}, u32[]{:S(2)}) collective-permute-start(f32[168,256]{1,0:T(8,128)S(1)} %get-tuple-element.25.mine_back), channel_id=1, source_target_pairs={{8,0},{24,16},{40,32},{56,48},{72,64},{88,80},{104,96},{120,112},{... | collective-permute-start | bytes 516104 | tf_op jit(solution)/shard_map/ppermute | solution.py:18
  12.2 19.7 %collective-permute-start.1 = (f32[88,256]{1,0:T(8,128)S(1)}, f32[88,256]{1,0:T(8,128)S(1)}, u32[]{:S(2)}, u32[]{:S(2)}) collective-permute-start(f32[88,256]{1,0:T(8,128)S(1)} %get-tuple-element.26.mine_ahead), channel_id=1, source_target_pairs={{0,8},{8,16},{16,24},{24,32},{32,40},{40,48},{48,56},{56,64},{64,7... | collective-permute-start | bytes 270344 | tf_op jit(solution)/shard_map/ppermute | solution.py:13
  20.4 9.1 %collective-permute-start.3 = (f32[84,256]{1,0:T(8,128)S(1)}, f32[84,256]{1,0:T(8,128)S(1)}, u32[]{:S(2)}, u32[]{:S(2)}) collective-permute-start(f32[84,256]{1,0:T(8,128)S(1)} %get-tuple-element.27), channel_id=1, source_target_pairs={{0,504},{16,8},{32,24},{48,40},{64,56},{80,72},{96,88},{112,104},{... | collective-permute-start | bytes 258056 | tf_op jit(solution)/shard_map/ppermute | solution.py:18
  27.4 2.8 %collective-permute-start.4 = (f32[84,256]{1,0:T(8,128)S(1)}, f32[84,256]{1,0:T(8,128)S(1)}, u32[]{:S(2)}, u32[]{:S(2)}) collective-permute-start(f32[84,256]{1,0:T(8,128)S(1)} %get-tuple-element.28), channel_id=1, source_target_pairs={{0,504},{16,8},{32,24},{48,40},{64,56},{80,72},{96,88},{112,104},{... | collective-permute-start | bytes 258056 | tf_op jit(solution)/shard_map/ppermute | solution.py:18

commit v4 on v3

--- a/solution.py
+++ b/solution.py
@@ -135,6 +135,39 @@
     return found
 
 
+OWN_TERMS = [
+    (cx, corner, partner, kind)
+    for cy in range(2)
+    for cx, corner, partners in ((0, 2 + cy, ((cy, "s"),)), (1, cy, None), (1, 2 + cy, None))
+    for partner, kind in (
+        partners
+        or (
+            ([(2 + cy, "s")] if corner < 2 else [])
+            + [(2 + cy, "o"), (3 - cy, "0"), (3 - cy, "1")]
+        )
+    )
+]
+
+
+def weigh_own(summer, elements, own_ref):
+    for place, (plane, corner, partner, kind) in enumerate(OWN_TERMS):
+        part = elements[plane][corner % 2]
+        for i in range(3):
+            for j in range(3):
+                own_ref[place * 9 + i * 3 + j] = part.modulus * summer.entry(part, corner, partner, kind, i, j)
+
+
+def own_force(own_ref, plane, corner, terms):
+    total = [None] * 3
+    for partner, kind, values in terms:
+        place = OWN_TERMS.index((plane, corner, partner, kind))
+        for i in range(3):
+            for j in range(3):
+                part = own_ref[place * 9 + i * 3 + j] * values[j]
+                total[i] = part if total[i] is None else total[i] + part
+    return total
+
+
 def added(left, right):
     return [a + b for a, b in zip(left, right)]
 
@@ -211,25 +244,33 @@
     return even, before
 
 
-def fetch_kernel(u_hbm, load_hbm, mod_hbm, phase_hbm, out_ref, u_ref, load_ref, mod_ref, phase_ref, sems):
+def started(sources, targets, sems):
     copies = [
         pltpu.make_async_copy(source, target, sems.at[k])
-        for k, (source, target) in enumerate(
-            ((u_hbm, u_ref), (mod_hbm, mod_ref), (phase_hbm, phase_ref), (load_hbm, load_ref))
-        )
+        for k, (source, target) in enumerate(zip(sources, targets))
     ]
     for copy in copies:
         copy.start()
-    for copy in copies[:3]:
+    return copies
+
+
+def rim_kernel(u_hbm, mod_hbm, phase_hbm, out_ref, u_ref, mod_ref, phase_ref, sems):
+    edge = pl.ds(u_hbm.shape[2] - 8, 8)
+    sources = (u_hbm.at[:, :, edge, :], mod_hbm.at[:, edge, :], phase_hbm.at[:, edge, :])
+    for copy in started(sources, (u_ref, mod_ref, phase_ref), sems):
         copy.wait()
-    last = u_ref.shape[2] - 1
     for plane in range(2):
         for c in range(3):
-            out_ref[3 * plane + c : 3 * plane + c + 1, :] = u_ref[c, plane, last : last + 1, :]
-        out_ref[6 + plane : 7 + plane, :] = mod_ref[plane, last : last + 1, :]
-        out_ref[8 + plane : 9 + plane, :] = phase_ref[plane, last : last + 1, :].astype(jnp.float32)
+            out_ref[3 * plane + c : 3 * plane + c + 1, :] = u_ref[c, plane, 7:8, :]
+        out_ref[6 + plane : 7 + plane, :] = mod_ref[plane, 7:8, :]
+        out_ref[8 + plane : 9 + plane, :] = phase_ref[plane, 7:8, :].astype(jnp.float32)
     out_ref[10:16, :] = jnp.zeros((6, out_ref.shape[1]), jnp.float32)
-    copies[3].wait()
+
+
+def fetch_kernel(u_hbm, load_hbm, mod_hbm, phase_hbm, u_ref, load_ref, mod_ref, phase_ref, sems):
+    targets = (u_ref, load_ref, mod_ref, phase_ref)
+    for copy in started((u_hbm, load_hbm, mod_hbm, phase_hbm), targets, sems):
+        copy.wait()
 
 
 def prepare_kernel(table, u_ref, load_ref, mod_ref, phase_ref, tiles_ref, back_ref, ahead_ref, work_ref):
@@ -313,13 +354,16 @@
     second_ref[...] = back_ref[first_ref.shape[0] :, :]
 
 
-def inner_kernel(tiles_ref, u_ref, load_ref, mod_ref, phase_ref, halo_ref, sums_ref, work_ref):
+def inner_kernel(tiles_ref, u_ref, load_ref, mod_ref, phase_ref, halo_ref, sums_ref, own_ref, work_ref):
     half, cols = u_ref.shape[2] // 2, u_ref.shape[3]
     summer, rows = Summer(tiles_ref), Rows(work_ref)
     zero = plane_views(*local_plane(rows, u_ref, halo_ref, 0))
     one = plane_views(*local_plane(rows, u_ref, halo_ref, 1))
     rows_zero = element_rows(rows, mod_ref, phase_ref, halo_ref, 0)
     rows_one = element_rows(rows, mod_ref, phase_ref, halo_ref, 1)
+    weigh_own(
+        summer, [[Elements(*pair) for pair in rows] for rows in (rows_zero, rows_one)], own_ref
+    )
     total, middle, first, last = None, None, None, None
     for cy in range(2):
         left, right = Elements(*rows_zero[cy]), Elements(*rows_one[cy])
@@ -351,55 +395,63 @@
     return [block, next_lane(block), jnp.concatenate([rest, next_lane(rest)], axis=0)]
 
 
-def finish_kernel(
-    tiles_ref, u_ref, mod_ref, phase_ref, halo_ref, sums_ref, mine_back, mine_ahead, ahead_ref, odd_ref, top_ref, end_ref, out_ref, work_ref
+def far_kernel(tiles_ref, sums_ref, own_ref, mine_ahead, odd_ref, top_ref, end_ref, out_ref):
+    half, cols = out_ref.shape[1:]
+    summer = Summer(tiles_ref)
+    back = jnp.concatenate([top_ref[...], end_ref[...]], axis=0) + odd_ref[...]
+    even_two = [back[c * half : (c + 1) * half] for c in range(3)]
+    odd_two = [back[(3 + c) * half : (4 + c) * half] for c in range(3)]
+    top_two = [back[10 * half + c : 10 * half + c + 1] for c in range(3)]
+    two = plane_views(even_two, odd_two, top_two)
+    after, upper, beyond = None, None, None
+    for cy in range(2):
+        start = (6 + cy) * half
+        plus = Elements(back[start : start + half], back[start + 2 * half : start + 3 * half])
+        part = own_force(own_ref, 1, 2 + cy, terms_of(two, 1, cy, 1, "o"))
+        after = part if after is None else added(after, part)
+        part = own_force(own_ref, 1, cy, terms_of(two, 0, cy, 1, "o"))
+        beyond = part if beyond is None else added(beyond, part)
+        part = summer.diagonal(plus, cy)
+        upper = part if upper is None else added(upper, part)
+    after, upper = at_nodes(after, cols), at_nodes(upper, cols)
+    sent = unpacked(mine_ahead, half)
+    right = [even_two[c] - sent[c] - after[c] for c in range(3)]
+    solved = applied(inverse_of([sums_ref[21 + k] + upper[k] for k in range(9)]), right)
+    far = [pair_even(a)["s"] for a in solved]
+    for cy in range(2):
+        beyond = added(beyond, own_force(own_ref, 1, cy, [(2 + cy, "s", far)]))
+    beyond = at_nodes(beyond, cols)
+    for c in range(3):
+        out_ref[c] = sums_ref[c] - beyond[c]
+
+
+def near_kernel(
+    tiles_ref, u_ref, halo_ref, sums_ref, own_ref, mine_back, ahead_ref, right_ref, out_ref, work_ref
 ):
     half, cols = u_ref.shape[2] // 2, u_ref.shape[3]
     quarter = half // 2
-    back_ref = jnp.concatenate([top_ref[...], end_ref[...]], axis=0) + odd_ref[...]
     summer, rows = Summer(tiles_ref), Rows(work_ref)
     even_zero, odd_zero, top_zero = local_plane(rows, u_ref, halo_ref, 0)
     zero = plane_views(even_zero, odd_zero, top_zero)
-    rows_zero = element_rows(rows, mod_ref, phase_ref, halo_ref, 0)
-    rows_one = element_rows(rows, mod_ref, phase_ref, halo_ref, 1)
-    even_two = [back_ref[c * half : (c + 1) * half, :] for c in range(3)]
-    odd_two = [back_ref[(3 + c) * half : (4 + c) * half, :] for c in range(3)]
-    top_two = [back_ref[10 * half + c : 10 * half + c + 1, :] for c in range(3)]
-    two = plane_views(even_two, odd_two, top_two)
     even = even_lanes((half, cols))
-    before, after, lower, upper, beyond = None, None, None, None, None
+    before, lower = None, None
     for cy in range(2):
         start = half + quarter + cy * half
         minus = Elements(ahead_ref[start : start + half, :], ahead_ref[start + 2 * half : start + 3 * half, :])
-        start = (6 + cy) * half
-        plus = Elements(back_ref[start : start + half, :], back_ref[start + 2 * half : start + 3 * half, :])
-        right = Elements(*rows_one[cy])
         part = summer.force(minus, 2 + cy, terms_of(zero, 1, cy, 1, "o"))
         before = part if before is None else added(before, part)
-        part = summer.force(right, 2 + cy, terms_of(two, 1, cy, 1, "o"))
-        after = part if after is None else added(after, part)
-        part = summer.force(right, cy, terms_of(two, 0, cy, 1, "o"))
-        beyond = part if beyond is None else added(beyond, part)
         part = summer.diagonal(minus, 2 + cy)
         lower = part if lower is None else added(lower, part)
-        part = summer.diagonal(plus, cy)
-        upper = part if upper is None else added(upper, part)
-    before, after = at_nodes(before, cols), at_nodes(after, cols)
-    lower, upper = at_nodes(lower, cols), at_nodes(upper, cols)
-    came, sent = unpacked(ahead_ref, half), unpacked(mine_ahead, half)
+    before, lower = at_nodes(before, cols), at_nodes(lower, cols)
+    came = unpacked(ahead_ref, half)
     right = [mine_back[c * half : (c + 1) * half, :] - came[c] - before[c] for c in range(3)]
     first_new = applied(inverse_of([sums_ref[12 + k] + lower[k] for k in range(9)]), right)
-    right = [even_two[c] - sent[c] - after[c] for c in range(3)]
-    third_new = applied(inverse_of([sums_ref[21 + k] + upper[k] for k in range(9)]), right)
     near = [pair_even(a)["s"] for a in first_new]
-    far = [pair_even(a)["s"] for a in third_new]
-    for cy in range(2):
-        left, right = Elements(*rows_zero[cy]), Elements(*rows_one[cy])
-        beyond = added(beyond, summer.force(left, 2 + cy, [(cy, "s", near)]))
-        beyond = added(beyond, summer.force(right, cy, [(2 + cy, "s", far)]))
+    beyond = own_force(own_ref, 0, 2, [(0, "s", near)])
+    beyond = added(beyond, own_force(own_ref, 0, 3, [(1, "s", near)]))
     beyond = at_nodes(beyond, cols)
-    solved = [sums_ref[3 + k] for k in range(9)]
-    second_new = applied(solved, [sums_ref[c] - beyond[c] for c in range(3)])
+    inverse = [sums_ref[3 + k] for k in range(9)]
+    second_new = applied(inverse, [right_ref[c] - beyond[c] for c in range(3)])
     for c in range(3):
         out_ref[c, 0] = rows.merge(jnp.where(even, first_new[c], even_zero[c]), odd_zero[c])
         own, other = rows.split(u_ref[c, 1])
@@ -420,16 +472,32 @@
     kind = displacement.dtype
     table = stiffness.reshape(-1)
     slots = 16
-    rim, displacement, load, element_modulus, element_phase = pl.pallas_call(
+    hbm = [
+        pltpu.with_memory_space_constraint(a, pltpu.HBM)
+        for a in (displacement, load, element_modulus, element_phase)
+    ]
+    rim = pl.pallas_call(
+        rim_kernel,
+        in_specs=[pl.BlockSpec(memory_space=pltpu.HBM)] * 3,
+        out_specs=whole(),
+        out_shape=jax.ShapeDtypeStruct((16, cols), kind),
+        scratch_shapes=[
+            pltpu.VMEM((3, planes, 8, cols), kind),
+            pltpu.VMEM((planes, 8, cols), kind),
+            pltpu.VMEM((planes, 8, cols), element_phase.dtype),
+            pltpu.SemaphoreType.DMA((3,)),
+        ],
+        compiler_params=pltpu.CompilerParams(vmem_limit_bytes=8 << 20),
+    )(hbm[0], hbm[2], hbm[3])
+    displacement, load, element_modulus, element_phase = pl.pallas_call(
         fetch_kernel,
-        in_specs=[pl.BlockSpec(memory_space=pl.ANY)] * 4,
-        out_specs=[whole()] * 5,
-        out_shape=[jax.ShapeDtypeStruct((16, cols), kind)]
-        + [jax.ShapeDtypeStruct(a.shape, a.dtype) for a in (displacement, load, element_modulus, element_phase)],
+        in_specs=[pl.BlockSpec(memory_space=pltpu.HBM)] * 4,
+        out_specs=[whole()] * 4,
+        out_shape=[jax.ShapeDtypeStruct(a.shape, a.dtype) for a in hbm],
         scratch_shapes=[pltpu.SemaphoreType.DMA((4,))],
         compiler_params=pltpu.CompilerParams(vmem_limit_bytes=8 << 20),
         cost_estimate=pl.CostEstimate(flops=1_000_000_000, bytes_accessed=0, transcendentals=0),
-    )(*(pltpu.with_memory_space_constraint(a, pltpu.HBM) for a in (displacement, load, element_modulus, element_phase)))
+    )(*hbm)
     halo = shifted(rim, "gy", 1)
     back_rows, ahead_rows = 10 * half + 8, 5 * half + half // 2
     params = pltpu.CompilerParams(vmem_limit_bytes=24 << 20)
@@ -457,25 +525,33 @@
     from_odd = shifted_from(back, "gx", -1, 1)
     from_last = shifted(ahead, "gx", 1)
     from_even = [shifted_from(part, "gx", -1, 0) for part in (top, end)]
-    sums = pl.pallas_call(
+    sums, own = pl.pallas_call(
         inner_kernel,
         in_specs=[whole()] * 6,
-        out_specs=whole(),
-        out_shape=jax.ShapeDtypeStruct((30, half, cols), kind),
+        out_specs=[whole()] * 2,
+        out_shape=[
+            jax.ShapeDtypeStruct((30, half, cols), kind),
+            jax.ShapeDtypeStruct((9 * len(OWN_TERMS), half * cols // 1024, 8, 128), kind),
+        ],
         scratch_shapes=scratch,
         compiler_params=params,
         cost_estimate=pl.CostEstimate(flops=20_000_000, bytes_accessed=1_000_000, transcendentals=0),
     )(coefficients, displacement, load, element_modulus, element_phase, halo)
+    right = pl.pallas_call(
+        far_kernel,
+        in_specs=[whole()] * 7,
+        out_specs=whole(),
+        out_shape=jax.ShapeDtypeStruct((3, half, cols), kind),
+        compiler_params=params,
+    )(coefficients, sums, own, ahead, from_odd, *from_even)
     return pl.pallas_call(
-        finish_kernel,
-        in_specs=[whole()] * 12,
+        near_kernel,
+        in_specs=[whole()] * 8,
         out_specs=whole(),
         out_shape=jax.ShapeDtypeStruct(displacement.shape, kind),
         scratch_shapes=scratch,
         compiler_params=params,
-    )(
-        coefficients, displacement, element_modulus, element_phase, halo, sums, back, ahead, from_last, from_odd, *from_even
-    )
+    )(coefficients, displacement, halo, sums, own, back, from_last, right)
 
 
 def solution(mesh):

time: 33.6 us -> 33.1 us (0.985)
  waiting for transfers between devices: 3.9 us -> 0.92 us
  starting transfers between devices: 23.2 us -> 24.3 us
  Pallas kernels: 5.51 us -> 6.59 us
    ppermute x2, waiting for transfers between devices: 3.16 us -> 0.47 us  [shifted(): lax.ppermute(x, axis, [(i, (i + by) % devices) for i in range(devices)])]
    ppermute x2, starting transfers between devices: 13.6 us -> 14.7 us  [shifted(): lax.ppermute(x, axis, [(i, (i + by) % devices) for i in range(devices)])]
    pallas_call x3 -> x5, Pallas kernels: 3.54 us -> 4.61 us  [the longest x1 1.13 us: on_device(): pl.pallas_call(near_kernel, in_specs=[whole()] * 8, out_specs=whole(), ou...]
  transfers between devices with their start and end apart: 5 -> 5, of which waited for: 3 -> 2; matrix products, arithmetic and copies ran while one was open for 2% -> 2% of each run, Pallas kernels for 8% -> 13%
where the time goes in v4:
time: 33.1 us; the launch traced here: 32.6 us
  starting transfers between devices  24.3 us (73%)
  Pallas kernels  6.59 us (20%)
  waiting for transfers between devices  0.92 us (3%)
  local copies, waits for them, and re-layouts  0.76 us (2%)
    ppermute x2, starting transfers between devices, shifted(): lax.ppermute(x, axis, [(i, (i + by) % devices) for i in range(devices)])  14.7 us
    ppermute x3, starting transfers between devices, shifted_from(): lax.ppermute(x, axis, [(i, (i + by) % devices) for i in range(parity, dev...  9.6 us
    pallas_call x1, Pallas kernels, on_device(): pl.pallas_call(prepare_kernel, in_specs=[scalars()] + [whole()] * 4, out_...  1.72 us
    pallas_call x1, Pallas kernels, on_device(): pl.pallas_call(near_kernel, in_specs=[whole()] * 8, out_specs=whole(), ou...  1.13 us
    pallas_call x1, Pallas kernels, on_device(): pl.pallas_call(fetch_kernel, in_specs=[pl.BlockSpec(memory_space=pltpu.HB...  1.1 us
    pallas_call x1, Pallas kernels, on_device(): pl.pallas_call(inner_kernel, in_specs=[whole()] * 6, out_specs=[whole()]...  1.08 us
    pallas_call x1, Pallas kernels, on_device(): pl.pallas_call(rim_kernel, in_specs=[pl.BlockSpec(memory_space=pltpu.HBM)...  0.87 us
  transfers between devices with their start and end apart: 5, of which 2 were waited for; matrix products, arithmetic and copies ran while one was open for 2% of the time, Pallas kernels for 13%

profile of v4, /device:TPU:1, one launch (start us, length us, event | category | flops | bytes accessed | tf_op | source)
XLA Modules:
  0.0 32.6 jit_solution(15398864703639834601)
XLA Ops:
  0.0 0.0 copy-start
  0.0 0.9 %shard_map.57 = f32[16,256]{1,0:T(8,128)S(1)} custom-call(f32[3,2,32,256]{3,2,1,0:T(8,128)} %u_hbm.3, f32[2,32,256]{2,1,0:T(8,128)} %mod_hbm.3, s32[2,32,256]{2,1,0:T(8,128)} %phase_hbm.3), custom_call_target="tpu_custom_call" | custom-call | tf_op jit(solution)/shard_map/pallas_call | solution.py:479
  0.9 5.4 %collective-permute-start = (f32[16,256]{1,0:T(8,128)S(1)}, f32[16,256]{1,0:T(8,128)S(1)}, u32[]{:S(2)}, u32[]{:S(2)}) collective-permute-start(f32[16,256]{1,0:T(8,128)S(1)} %shard_map.57), channel_id=1, source_target_pairs={{0,1},{1,2},{2,3},{3,4},{4,5},{5,6},{6,7},{7,0},{8,9},{9,10},{10,1... | collective-permute-start | bytes 49160 | tf_op jit(solution)/shard_map/ppermute | solution.py:13
  6.3 1.1 %shard_map.55 = (f32[3,2,32,256]{3,2,1,0:T(8,128)S(1)}, f32[3,2,32,256]{3,2,1,0:T(8,128)S(1)}, f32[2,32,256]{2,1,0:T(8,128)S(1)}, s32[2,32,256]{2,1,0:T(8,128)S(1)}) custom-call(f32[3,2,32,256]{3,2,1,0:T(8,128)} %u_hbm.3, f32[3,2,32,256]{3,2,1,0:T(8,128)} %load_hbm.1, f32[2,32,256]{2,1,0:T(8,128)} %mod_hbm.3, s32[2,32,256]{2,1,0:T(8,128)} %phase_hbm.3), custom_call_target="tpu_custom_call" | custom-call | flops 1000000000 | tf_op jit(solution)/shard_map/pallas_call | solution.py:492
  7.4 0.0 copy-done
  7.4 0.5 %copy.6 = f32[3,8,8,3,3]{4,3,2,1,0:T(4,128)S(1)} copy(f32[3,8,8,3,3]{2,1,4,3,0:T(8,128)S(1)} %copy-done) | data formatting | bytes 13824 | tf_op args[4]
  7.9 0.3 reshape.3.table
  8.1 1.7 %shard_map.56 = (f32[864,8,128]{2,1,0:T(8,128)S(1)}, f32[168,256]{1,0:T(8,128)S(1)}, f32[88,256]{1,0:T(8,128)S(1)}) custom-call(f32[1728]{0:T(1024)S(1)} %reshape.3.table, f32[3,2,32,256]{3,2,1,0:T(8,128)S(1)} %get-tuple-element.18.u_ref, f32[3,2,32,256]{3,2,1,0:T(8,128)S(1)} %get-tuple-element.19.load_ref, f32[2,32,256]{2,1,0:T(8,128)S(1)} %get-tuple-element.20.mod_ref, ...), custom_call_target="tpu_custom_call" | custom-call | flops 20000000 | bytes 6000000 | tf_op jit(solution)/shard_map/pallas_call | solution.py:509
  9.9 0.5 %collective-permute-done.halo_ref = f32[16,256]{1,0:T(8,128)S(1)} collective-permute-done((f32[16,256]{1,0:T(8,128)S(1)}, f32[16,256]{1,0:T(8,128)S(1)}, u32[]{:S(2)}, u32[]{:S(2)}) %collective-permute-start) | collective-permute-done | bytes 16416 | tf_op jit(solution)/shard_map/ppermute | solution.py:13
  10.3 0.3 shard_map.59
  10.6 1.3 %collective-permute-start.2 = (f32[168,256]{1,0:T(8,128)S(1)}, f32[168,256]{1,0:T(8,128)S(1)}, u32[]{:S(2)}, u32[]{:S(2)}) collective-permute-start(f32[168,256]{1,0:T(8,128)S(1)} %get-tuple-element.27.mine_back), channel_id=1, source_target_pairs={{8,0},{24,16},{40,32},{56,48},{72,64},{88,80},{104,96},{120,112},{... | collective-permute-start | bytes 516104 | tf_op jit(solution)/shard_map/ppermute | solution.py:18
  11.9 9.3 %collective-permute-start.1 = (f32[88,256]{1,0:T(8,128)S(1)}, f32[88,256]{1,0:T(8,128)S(1)}, u32[]{:S(2)}, u32[]{:S(2)}) collective-permute-start(f32[88,256]{1,0:T(8,128)S(1)} %get-tuple-element.28.mine_ahead), channel_id=1, source_target_pairs={{0,8},{8,16},{16,24},{24,32},{32,40},{40,48},{48,56},{56,64},{64,7... | collective-permute-start | bytes 270344 | tf_op jit(solution)/shard_map/ppermute | solution.py:13
  21.2 7.0 %collective-permute-start.3 = (f32[84,256]{1,0:T(8,128)S(1)}, f32[84,256]{1,0:T(8,128)S(1)}, u32[]{:S(2)}, u32[]{:S(2)}) collective-permute-start(f32[84,256]{1,0:T(8,128)S(1)} %get-tuple-element.29), channel_id=1, source_target_pairs={{0,504},{16,8},{32,24},{48,40},{64,56},{80,72},{96,88},{112,104},{... | collective-permute-start | bytes 258056 | tf_op jit(solution)/shard_map/ppermute | solution.py:18
  28.2 1.3 %collective-permute-start.4 = (f32[84,256]{1,0:T(8,128)S(1)}, f32[84,256]{1,0:T(8,128)S(1)}, u32[]{:S(2)}, u32[]{:S(2)}) collective-permute-start(f32[84,256]{1,0:T(8,128)S(1)} %get-tuple-element.30), channel_id=1, source_target_pairs={{0,504},{16,8},{32,24},{48,40},{64,56},{80,72},{96,88},{112,104},{... | collective-permute-start | bytes 258056 | tf_op jit(solution)/shard_map/ppermute | solution.py:18
  29.5 1.1 %shard_map.58 = (f32[30,16,256]{2,1,0:T(8,128)S(1)}, f32[144,4,8,128]{3,2,1,0:T(8,128)S(1)}) custom-call(f32[864,8,128]{2,1,0:T(8,128)S(1)} %get-tuple-element.22.tiles_ref, f32[3,2,32,256]{3,2,1,0:T(8,128)S(1)} %get-tuple-element.18.u_ref, f32[3,2,32,256]{3,2,1,0:T(8,128)S(1)} %get-tuple-element.19.load_ref, f32[2,32,256]{2,1,0:T(8,128)S(1)} %get-tuple-element.20.mod_ref, ...), custom_call_target="tpu_custom_call" | custom-call | flops 20000000 | bytes 1000000 | tf_op jit(solution)/shard_map/pallas_call | solution.py:528
  30.6 0.0 collective-permute-done.3.top_ref
  30.6 0.4 %collective-permute-done.4.end_ref = f32[84,256]{1,0:T(8,128)S(1)} collective-permute-done((f32[84,256]{1,0:T(8,128)S(1)}, f32[84,256]{1,0:T(8,128)S(1)}, u32[]{:S(2)}, u32[]{:S(2)}) %collective-permute-start.4) | collective-permute-done | bytes 86048 | tf_op jit(solution)/shard_map/ppermute | solution.py:18
  31.1 0.0 collective-permute-done.2.odd_ref
  31.1 0.4 %shard_map.60.right_ref = f32[3,16,256]{2,1,0:T(8,128)S(1)} custom-call(f32[864,8,128]{2,1,0:T(8,128)S(1)} %get-tuple-element.22.tiles_ref, f32[30,16,256]{2,1,0:T(8,128)S(1)} %get-tuple-element.23.sums_ref, f32[144,4,8,128]{3,2,1,0:T(8,128)S(1)} %get-tuple-element.24.own_ref, f32[88,256]{1,0:T(8,128)S(1)} %get-tuple-element.28.mine_ahead, ...), custom_call_target="tpu_custom_call" | custom-call | tf_op jit(solution)/shard_map/pallas_call | solution.py:540
  31.5 0.0 collective-permute-done.1.ahead_ref
  31.5 1.1 %shard_map.61 = f32[3,2,32,256]{3,2,1,0:T(8,128)} custom-call(f32[864,8,128]{2,1,0:T(8,128)S(1)} %get-tuple-element.22.tiles_ref, f32[3,2,32,256]{3,2,1,0:T(8,128)S(1)} %get-tuple-element.18.u_ref, f32[16,256]{1,0:T(8,128)S(1)} %collective-permute-done.halo_ref, f32[30,16,256]{2,1,0:T(8,128)S(1)} %get-tuple-element.23.sums_ref, ...), custom_call_target="tpu_custom_call" | custom-call | tf_op jit(solution)/shard_map/pallas_call | solution.py:547
Async XLA Ops:
  0.0 7.4 %copy-start = (f32[3,8,8,3,3]{2,1,4,3,0:T(8,128)S(1)}, f32[3,8,8,3,3]{2,1,4,3,0:T(8,128)}, u32[]{:S(2)}) copy-start(f32[3,8,8,3,3]{2,1,4,3,0:T(8,128)} %param.9) | copy-start | bytes 20740
  0.9 9.5 %collective-permute-start = (f32[16,256]{1,0:T(8,128)S(1)}, f32[16,256]{1,0:T(8,128)S(1)}, u32[]{:S(2)}, u32[]{:S(2)}) collective-permute-start(f32[16,256]{1,0:T(8,128)S(1)} %shard_map.57), channel_id=1, source_target_pairs={{0,1},{1,2},{2,3},{3,4},{4,5},{5,6},{6,7},{7,0},{8,9},{9,10},{10,1... | collective-permute-start | bytes 49160 | tf_op jit(solution)/shard_map/ppermute | solution.py:13
  10.6 20.5 %collective-permute-start.2 = (f32[168,256]{1,0:T(8,128)S(1)}, f32[168,256]{1,0:T(8,128)S(1)}, u32[]{:S(2)}, u32[]{:S(2)}) collective-permute-start(f32[168,256]{1,0:T(8,128)S(1)} %get-tuple-element.27.mine_back), channel_id=1, source_target_pairs={{8,0},{24,16},{40,32},{56,48},{72,64},{88,80},{104,96},{120,112},{... | collective-permute-start | bytes 516104 | tf_op jit(solution)/shard_map/ppermute | solution.py:18
  11.9 19.6 %collective-permute-start.1 = (f32[88,256]{1,0:T(8,128)S(1)}, f32[88,256]{1,0:T(8,128)S(1)}, u32[]{:S(2)}, u32[]{:S(2)}) collective-permute-start(f32[88,256]{1,0:T(8,128)S(1)} %get-tuple-element.28.mine_ahead), channel_id=1, source_target_pairs={{0,8},{8,16},{16,24},{24,32},{32,40},{40,48},{48,56},{56,64},{64,7... | collective-permute-start | bytes 270344 | tf_op jit(solution)/shard_map/ppermute | solution.py:13
  21.2 9.4 %collective-permute-start.3 = (f32[84,256]{1,0:T(8,128)S(1)}, f32[84,256]{1,0:T(8,128)S(1)}, u32[]{:S(2)}, u32[]{:S(2)}) collective-permute-start(f32[84,256]{1,0:T(8,128)S(1)} %get-tuple-element.29), channel_id=1, source_target_pairs={{0,504},{16,8},{32,24},{48,40},{64,56},{80,72},{96,88},{112,104},{... | collective-permute-start | bytes 258056 | tf_op jit(solution)/shard_map/ppermute | solution.py:18
  28.2 2.8 %collective-permute-start.4 = (f32[84,256]{1,0:T(8,128)S(1)}, f32[84,256]{1,0:T(8,128)S(1)}, u32[]{:S(2)}, u32[]{:S(2)}) collective-permute-start(f32[84,256]{1,0:T(8,128)S(1)} %get-tuple-element.30), channel_id=1, source_target_pairs={{0,504},{16,8},{32,24},{48,40},{64,56},{80,72},{96,88},{112,104},{... | collective-permute-start | bytes 258056 | tf_op jit(solution)/shard_map/ppermute | solution.py:18

commit v5 on v4

--- a/solution.py
+++ b/solution.py
@@ -351,7 +351,8 @@
         even, ahead_in[half : half + 1, :] + beyond[2][0:1], ahead_in[half : half + 1, :]
     )
     first_ref[...] = back_ref[: first_ref.shape[0], :]
-    second_ref[...] = back_ref[first_ref.shape[0] :, :]
+    cut = first_ref.shape[0]
+    second_ref[...] = back_ref[cut : cut + second_ref.shape[0], :]
 
 
 def inner_kernel(tiles_ref, u_ref, load_ref, mod_ref, phase_ref, halo_ref, sums_ref, own_ref, work_ref):
@@ -398,7 +399,8 @@
 def far_kernel(tiles_ref, sums_ref, own_ref, mine_ahead, odd_ref, top_ref, end_ref, out_ref):
     half, cols = out_ref.shape[1:]
     summer = Summer(tiles_ref)
-    back = jnp.concatenate([top_ref[...], end_ref[...]], axis=0) + odd_ref[...]
+    back = jnp.concatenate([top_ref[...], end_ref[...]], axis=0)
+    back = back + odd_ref[: back.shape[0], :]
     even_two = [back[c * half : (c + 1) * half] for c in range(3)]
     odd_two = [back[(3 + c) * half : (4 + c) * half] for c in range(3)]
     top_two = [back[10 * half + c : 10 * half + c + 1] for c in range(3)]
@@ -504,7 +506,7 @@
     scratch = [pltpu.VMEM((slots, cols // 128, rows, 128), kind)]
     ahead_shape = jax.ShapeDtypeStruct((ahead_rows, cols), kind)
     back_shape = jax.ShapeDtypeStruct((back_rows, cols), kind)
-    part_shape = jax.ShapeDtypeStruct((back_rows // 2, cols), kind)
+    part_shapes = [jax.ShapeDtypeStruct((5 * half + k, cols), kind) for k in (0, 4)]
     tile_shape = jax.ShapeDtypeStruct((3 * PHASE_ROWS, 8, 128), kind)
     coefficients, back, ahead = pl.pallas_call(
         prepare_kernel,
@@ -519,7 +521,7 @@
         top_kernel,
         in_specs=[whole()] * 5,
         out_specs=[whole()] * 4,
-        out_shape=[back_shape, ahead_shape, part_shape, part_shape],
+        out_shape=[back_shape, ahead_shape, *part_shapes],
         compiler_params=params,
     )(coefficients, displacement, halo, back, ahead)
     from_odd = shifted_from(back, "gx", -1, 1)

time: 33.1 us -> 32.9 us (level)
  no operation moved by 1% of the time
where the time goes in v5:
time: 32.9 us; the launch traced here: 32.6 us
  starting transfers between devices  24.3 us (74%)
  Pallas kernels  6.59 us (20%)
  waiting for transfers between devices  0.85 us (3%)
  local copies, waits for them, and re-layouts  0.76 us (2%)
    ppermute x2, starting transfers between devices, shifted(): lax.ppermute(x, axis, [(i, (i + by) % devices) for i in range(devices)])  14.7 us
    ppermute x3, starting transfers between devices, shifted_from(): lax.ppermute(x, axis, [(i, (i + by) % devices) for i in range(parity, dev...  9.6 us
    pallas_call x1, Pallas kernels, on_device(): pl.pallas_call(prepare_kernel, in_specs=[scalars()] + [whole()] * 4, out_...  1.72 us
    pallas_call x1, Pallas kernels, on_device(): pl.pallas_call(near_kernel, in_specs=[whole()] * 8, out_specs=whole(), ou...  1.13 us
    pallas_call x1, Pallas kernels, on_device(): pl.pallas_call(fetch_kernel, in_specs=[pl.BlockSpec(memory_space=pltpu.HB...  1.1 us
    pallas_call x1, Pallas kernels, on_device(): pl.pallas_call(inner_kernel, in_specs=[whole()] * 6, out_specs=[whole()]...  1.08 us
    pallas_call x1, Pallas kernels, on_device(): pl.pallas_call(rim_kernel, in_specs=[pl.BlockSpec(memory_space=pltpu.HBM)...  0.87 us
  transfers between devices with their start and end apart: 5, of which 2 were waited for; matrix products, arithmetic and copies ran while one was open for 2% of the time, Pallas kernels for 13%

profile of v5, /device:TPU:1, one launch (start us, length us, event | category | flops | bytes accessed | tf_op | source)
XLA Modules:
  0.0 32.6 jit_solution(15224880239657036681)
XLA Ops:
  0.0 0.0 copy-start
  0.0 0.9 %shard_map.57 = f32[16,256]{1,0:T(8,128)S(1)} custom-call(f32[3,2,32,256]{3,2,1,0:T(8,128)} %u_hbm.3, f32[2,32,256]{2,1,0:T(8,128)} %mod_hbm.3, s32[2,32,256]{2,1,0:T(8,128)} %phase_hbm.3), custom_call_target="tpu_custom_call" | custom-call | tf_op jit(solution)/shard_map/pallas_call | solution.py:481
  0.9 5.4 %collective-permute-start = (f32[16,256]{1,0:T(8,128)S(1)}, f32[16,256]{1,0:T(8,128)S(1)}, u32[]{:S(2)}, u32[]{:S(2)}) collective-permute-start(f32[16,256]{1,0:T(8,128)S(1)} %shard_map.57), channel_id=1, source_target_pairs={{0,1},{1,2},{2,3},{3,4},{4,5},{5,6},{6,7},{7,0},{8,9},{9,10},{10,1... | collective-permute-start | bytes 49160 | tf_op jit(solution)/shard_map/ppermute | solution.py:13
  6.3 1.1 %shard_map.55 = (f32[3,2,32,256]{3,2,1,0:T(8,128)S(1)}, f32[3,2,32,256]{3,2,1,0:T(8,128)S(1)}, f32[2,32,256]{2,1,0:T(8,128)S(1)}, s32[2,32,256]{2,1,0:T(8,128)S(1)}) custom-call(f32[3,2,32,256]{3,2,1,0:T(8,128)} %u_hbm.3, f32[3,2,32,256]{3,2,1,0:T(8,128)} %load_hbm.1, f32[2,32,256]{2,1,0:T(8,128)} %mod_hbm.3, s32[2,32,256]{2,1,0:T(8,128)} %phase_hbm.3), custom_call_target="tpu_custom_call" | custom-call | flops 1000000000 | tf_op jit(solution)/shard_map/pallas_call | solution.py:494
  7.4 0.0 copy-done
  7.4 0.5 %copy.6 = f32[3,8,8,3,3]{4,3,2,1,0:T(4,128)S(1)} copy(f32[3,8,8,3,3]{2,1,4,3,0:T(8,128)S(1)} %copy-done) | data formatting | bytes 13824 | tf_op args[4]
  7.9 0.3 reshape.3.table
  8.1 1.7 %shard_map.56 = (f32[864,8,128]{2,1,0:T(8,128)S(1)}, f32[168,256]{1,0:T(8,128)S(1)}, f32[88,256]{1,0:T(8,128)S(1)}) custom-call(f32[1728]{0:T(1024)S(1)} %reshape.3.table, f32[3,2,32,256]{3,2,1,0:T(8,128)S(1)} %get-tuple-element.18.u_ref, f32[3,2,32,256]{3,2,1,0:T(8,128)S(1)} %get-tuple-element.19.load_ref, f32[2,32,256]{2,1,0:T(8,128)S(1)} %get-tuple-element.20.mod_ref, ...), custom_call_target="tpu_custom_call" | custom-call | flops 20000000 | bytes 6000000 | tf_op jit(solution)/shard_map/pallas_call | solution.py:511
  9.9 0.5 %collective-permute-done.halo_ref = f32[16,256]{1,0:T(8,128)S(1)} collective-permute-done((f32[16,256]{1,0:T(8,128)S(1)}, f32[16,256]{1,0:T(8,128)S(1)}, u32[]{:S(2)}, u32[]{:S(2)}) %collective-permute-start) | collective-permute-done | bytes 16416 | tf_op jit(solution)/shard_map/ppermute | solution.py:13
  10.3 0.3 shard_map.59
  10.6 1.3 %collective-permute-start.2 = (f32[168,256]{1,0:T(8,128)S(1)}, f32[168,256]{1,0:T(8,128)S(1)}, u32[]{:S(2)}, u32[]{:S(2)}) collective-permute-start(f32[168,256]{1,0:T(8,128)S(1)} %get-tuple-element.27.mine_back), channel_id=1, source_target_pairs={{8,0},{24,16},{40,32},{56,48},{72,64},{88,80},{104,96},{120,112},{... | collective-permute-start | bytes 516104 | tf_op jit(solution)/shard_map/ppermute | solution.py:18
  11.9 9.3 %collective-permute-start.1 = (f32[88,256]{1,0:T(8,128)S(1)}, f32[88,256]{1,0:T(8,128)S(1)}, u32[]{:S(2)}, u32[]{:S(2)}) collective-permute-start(f32[88,256]{1,0:T(8,128)S(1)} %get-tuple-element.28.mine_ahead), channel_id=1, source_target_pairs={{0,8},{8,16},{16,24},{24,32},{32,40},{40,48},{48,56},{56,64},{64,7... | collective-permute-start | bytes 270344 | tf_op jit(solution)/shard_map/ppermute | solution.py:13
  21.2 7.0 %collective-permute-start.4 = (f32[84,256]{1,0:T(8,128)S(1)}, f32[84,256]{1,0:T(8,128)S(1)}, u32[]{:S(2)}, u32[]{:S(2)}) collective-permute-start(f32[84,256]{1,0:T(8,128)S(1)} %get-tuple-element.30), channel_id=1, source_target_pairs={{0,504},{16,8},{32,24},{48,40},{64,56},{80,72},{96,88},{112,104},{... | collective-permute-start | bytes 258056 | tf_op jit(solution)/shard_map/ppermute | solution.py:18
  28.2 1.3 %collective-permute-start.3 = (f32[80,256]{1,0:T(8,128)S(1)}, f32[80,256]{1,0:T(8,128)S(1)}, u32[]{:S(2)}, u32[]{:S(2)}) collective-permute-start(f32[80,256]{1,0:T(8,128)S(1)} %get-tuple-element.29), channel_id=1, source_target_pairs={{0,504},{16,8},{32,24},{48,40},{64,56},{80,72},{96,88},{112,104},{... | collective-permute-start | bytes 245768 | tf_op jit(solution)/shard_map/ppermute | solution.py:18
  29.5 1.1 %shard_map.58 = (f32[30,16,256]{2,1,0:T(8,128)S(1)}, f32[144,4,8,128]{3,2,1,0:T(8,128)S(1)}) custom-call(f32[864,8,128]{2,1,0:T(8,128)S(1)} %get-tuple-element.22.tiles_ref, f32[3,2,32,256]{3,2,1,0:T(8,128)S(1)} %get-tuple-element.18.u_ref, f32[3,2,32,256]{3,2,1,0:T(8,128)S(1)} %get-tuple-element.19.load_ref, f32[2,32,256]{2,1,0:T(8,128)S(1)} %get-tuple-element.20.mod_ref, ...), custom_call_target="tpu_custom_call" | custom-call | flops 20000000 | bytes 1000000 | tf_op jit(solution)/shard_map/pallas_call | solution.py:530
  30.6 0.4 %collective-permute-done.3.top_ref = f32[80,256]{1,0:T(8,128)S(1)} collective-permute-done((f32[80,256]{1,0:T(8,128)S(1)}, f32[80,256]{1,0:T(8,128)S(1)}, u32[]{:S(2)}, u32[]{:S(2)}) %collective-permute-start.3) | collective-permute-done | bytes 81952 | tf_op jit(solution)/shard_map/ppermute | solution.py:18
  31.0 0.0 collective-permute-done.4.end_ref
  31.0 0.0 collective-permute-done.2.odd_ref
  31.0 0.4 %shard_map.60.right_ref = f32[3,16,256]{2,1,0:T(8,128)S(1)} custom-call(f32[864,8,128]{2,1,0:T(8,128)S(1)} %get-tuple-element.22.tiles_ref, f32[30,16,256]{2,1,0:T(8,128)S(1)} %get-tuple-element.23.sums_ref, f32[144,4,8,128]{3,2,1,0:T(8,128)S(1)} %get-tuple-element.24.own_ref, f32[88,256]{1,0:T(8,128)S(1)} %get-tuple-element.28.mine_ahead, ...), custom_call_target="tpu_custom_call" | custom-call | tf_op jit(solution)/shard_map/pallas_call | solution.py:542
  31.4 0.0 collective-permute-done.1.ahead_ref
  31.4 1.1 %shard_map.61 = f32[3,2,32,256]{3,2,1,0:T(8,128)} custom-call(f32[864,8,128]{2,1,0:T(8,128)S(1)} %get-tuple-element.22.tiles_ref, f32[3,2,32,256]{3,2,1,0:T(8,128)S(1)} %get-tuple-element.18.u_ref, f32[16,256]{1,0:T(8,128)S(1)} %collective-permute-done.halo_ref, f32[30,16,256]{2,1,0:T(8,128)S(1)} %get-tuple-element.23.sums_ref, ...), custom_call_target="tpu_custom_call" | custom-call | tf_op jit(solution)/shard_map/pallas_call | solution.py:549
Async XLA Ops:
  0.0 7.4 %copy-start = (f32[3,8,8,3,3]{2,1,4,3,0:T(8,128)S(1)}, f32[3,8,8,3,3]{2,1,4,3,0:T(8,128)}, u32[]{:S(2)}) copy-start(f32[3,8,8,3,3]{2,1,4,3,0:T(8,128)} %param.9) | copy-start | bytes 20740
  0.9 9.5 %collective-permute-start = (f32[16,256]{1,0:T(8,128)S(1)}, f32[16,256]{1,0:T(8,128)S(1)}, u32[]{:S(2)}, u32[]{:S(2)}) collective-permute-start(f32[16,256]{1,0:T(8,128)S(1)} %shard_map.57), channel_id=1, source_target_pairs={{0,1},{1,2},{2,3},{3,4},{4,5},{5,6},{6,7},{7,0},{8,9},{9,10},{10,1... | collective-permute-start | bytes 49160 | tf_op jit(solution)/shard_map/ppermute | solution.py:13
  10.6 20.4 %collective-permute-start.2 = (f32[168,256]{1,0:T(8,128)S(1)}, f32[168,256]{1,0:T(8,128)S(1)}, u32[]{:S(2)}, u32[]{:S(2)}) collective-permute-start(f32[168,256]{1,0:T(8,128)S(1)} %get-tuple-element.27.mine_back), channel_id=1, source_target_pairs={{8,0},{24,16},{40,32},{56,48},{72,64},{88,80},{104,96},{120,112},{... | collective-permute-start | bytes 516104 | tf_op jit(solution)/shard_map/ppermute | solution.py:18
  11.9 19.5 %collective-permute-start.1 = (f32[88,256]{1,0:T(8,128)S(1)}, f32[88,256]{1,0:T(8,128)S(1)}, u32[]{:S(2)}, u32[]{:S(2)}) collective-permute-start(f32[88,256]{1,0:T(8,128)S(1)} %get-tuple-element.28.mine_ahead), channel_id=1, source_target_pairs={{0,8},{8,16},{16,24},{24,32},{32,40},{40,48},{48,56},{56,64},{64,7... | collective-permute-start | bytes 270344 | tf_op jit(solution)/shard_map/ppermute | solution.py:13
  21.2 9.8 %collective-permute-start.4 = (f32[84,256]{1,0:T(8,128)S(1)}, f32[84,256]{1,0:T(8,128)S(1)}, u32[]{:S(2)}, u32[]{:S(2)}) collective-permute-start(f32[84,256]{1,0:T(8,128)S(1)} %get-tuple-element.30), channel_id=1, source_target_pairs={{0,504},{16,8},{32,24},{48,40},{64,56},{80,72},{96,88},{112,104},{... | collective-permute-start | bytes 258056 | tf_op jit(solution)/shard_map/ppermute | solution.py:18
  28.2 2.8 %collective-permute-start.3 = (f32[80,256]{1,0:T(8,128)S(1)}, f32[80,256]{1,0:T(8,128)S(1)}, u32[]{:S(2)}, u32[]{:S(2)}) collective-permute-start(f32[80,256]{1,0:T(8,128)S(1)} %get-tuple-element.29), channel_id=1, source_target_pairs={{0,504},{16,8},{32,24},{48,40},{64,56},{80,72},{96,88},{112,104},{... | collective-permute-start | bytes 245768 | tf_op jit(solution)/shard_map/ppermute | solution.py:18
